TPU v7x, 32 devices: a whole 2x2x4 slice. The times are simulated.
32 devices in a mesh: rows: 16 (over z, x, core), cols: 2 (over y).
Axes of the slice: x: 2, y: 2, z: 4, core: 2. Of those that a mesh axis runs over, the one named last changes fastest.
Arguments:
- matrix_blocks: bfloat16 [1024, 64, 1728], P(('rows', 'cols')), may hold values from -0.75 to 0.75
- restrict: bfloat16 [1024, 4096], P(('rows', 'cols')), may hold values from -1.5 to 1.5
- columns: int32 [1024, 27], P(('rows', 'cols')), may hold values from 0 to 191
- counts: int32 [1024], P(('rows', 'cols')), may hold values from 8 to 27, as said below
- aggregate: int32 [1024], P(('rows', 'cols')), may hold values from 0 to 1
Outputs:
- coarse: float32 [64, 64, 768], P(('rows', 'cols'))
Inputs may be any that keep to these rules, and one draw needn't show every extreme that they name: `counts`: used slots are the first ones of a row; some row uses all 27.
All inputs are finite; a program needn't handle non-finite values.
Results may differ from a plain program's by a relative error of at most 0.0029.
Values may be sent and summed in bfloat16 or wider, within the bound.
No kernel may reach another device: no remote copies, remote signals or barrier semaphores. Data moves between devices by JAX's collectives and lax.ppermute only.
A program may use at most 192 MiB of HBM per device.

v0:
```python
import jax
import jax.numpy as jnp
from jax import lax
from jax.sharding import PartitionSpec as P

BLK = 64
SLOTS = 27
ROWS_DEV = 32
AGG_DEV = 2


def padded(block, sides, width):
    for axis, dim in sides:
        count = lax.axis_size(axis)
        forward = [(i, i + 1) for i in range(count - 1)]
        backward = [(target, source) for source, target in forward]
        low = lax.ppermute(
            lax.slice_in_dim(block, block.shape[dim] - width, None, axis=dim), axis, forward
        )
        high = lax.ppermute(lax.slice_in_dim(block, 0, width, axis=dim), axis, backward)
        block = jnp.concatenate([low, block, high], axis=dim)
    return block


def per_device(matrix_blocks, restrict, columns, counts, aggregate):
    col_count = lax.axis_size("cols")
    row_count = lax.axis_size("rows")
    slab_index = lax.axis_index("rows")
    slab_rows = ROWS_DEV * col_count
    window = 3 * AGG_DEV * col_count
    slab_blocks, slab_aggs = (
        lax.all_gather(restrict, "cols", axis=0, tiled=True),
        lax.all_gather(aggregate, "cols", axis=0, tiled=True),
    )
    near_blocks, near_aggs = (
        padded(slab_blocks, (("rows", 0),), slab_rows),
        padded(slab_aggs, (("rows", 0),), slab_rows),
    )
    slot_index = jnp.arange(SLOTS, dtype=jnp.int32)
    inside = ((columns >= slab_rows) | (slab_index > 0)) & (
        (columns < 2 * slab_rows) | (slab_index < row_count - 1)
    )
    live_mask = ((slot_index[None, :] < counts[:, None]) & inside).astype(jnp.float32)
    slot_ids = columns // ROWS_DEV * AGG_DEV + near_aggs[columns]
    segment = aggregate[:, None] * window + slot_ids
    targets = jnp.arange(AGG_DEV * window, dtype=jnp.int32)
    one_hot = (segment[:, :, None] == targets[None, None, :]).astype(jnp.float32) * live_mask[
        :, :, None
    ]
    own_blocks = restrict.reshape(ROWS_DEV, BLK, BLK)
    left_prod = jnp.einsum(
        "ips,isn->ipn", own_blocks, matrix_blocks, preferred_element_type=jnp.float32
    )
    left_prod = left_prod.astype(jnp.bfloat16).reshape(ROWS_DEV, BLK, SLOTS, BLK)
    far_blocks = near_blocks[columns.reshape(-1)].reshape(ROWS_DEV, SLOTS, BLK, BLK)
    products = jnp.einsum(
        "ipks,ikqs->ikpq", left_prod, far_blocks, preferred_element_type=jnp.float32
    )
    summed = jnp.einsum(
        "ikm,ikpq->mpq",
        one_hot,
        products,
        precision=lax.Precision.HIGHEST,
        preferred_element_type=jnp.float32,
    )
    return (
        summed.reshape(AGG_DEV, window, BLK, BLK)
        .transpose(0, 2, 1, 3)
        .reshape(AGG_DEV, BLK, window * BLK)
    )


def solution(mesh):
    return jax.shard_map(
        per_device,
        mesh=mesh,
        in_specs=(
            P(("rows", "cols"), None, None),
            P(("rows", "cols"), None),
            P(("rows", "cols"), None),
            P(("rows", "cols")),
            P(("rows", "cols")),
        ),
        out_specs=P(("rows", "cols"), None, None),
        check_vma=False,
    )
```

profile of v0, /device:TPU:1, one launch (start us, length us, event | category | flops | bytes accessed | tf_op | source)
XLA Modules:
  0.0 161.4 jit_solution(17995716000623108469)
XLA Ops:
  0.0 9.0 %all_gather.7 = bf16[64,4096]{1,0:T(8,128)(2,1)S(1)} all-gather(bf16[32,4096]{1,0:T(8,128)(2,1)} %param.6), channel_id=1, replica_groups=mesh['rows'=16,'cols'=2] {'cols'}, dimensions={0}, use_global_device_ids=true | all-gather | bytes 786432 | tf_op jit(solution)/shard_map/all_gather | solution.py:32
  9.0 3.1 %collective-permute-start.3 = (bf16[64,4096]{1,0:T(8,128)(2,1)S(1)}, bf16[64,4096]{1,0:T(8,128)(2,1)S(1)}, u32[]{:S(2)}, u32[]{:S(2)}) collective-permute-start(bf16[64,4096]{1,0:T(8,128)(2,1)S(1)} %all_gather.7), channel_id=1, source_target_pairs={{2,0},{4,2},{6,4},{8,6},{10,8},{12,10},{14,12},{16,14},{18,16},{20... | collective-permute-start | bytes 1572872 | tf_op jit(solution)/shard_map/ppermute | solution.py:20
  12.2 3.2 %collective-permute-start.2 = (bf16[64,4096]{1,0:T(8,128)(2,1)S(1)}, bf16[64,4096]{1,0:T(8,128)(2,1)S(1)}, u32[]{:S(2)}, u32[]{:S(2)}) collective-permute-start(bf16[64,4096]{1,0:T(8,128)(2,1)S(1)} %all_gather.7), channel_id=1, source_target_pairs={{0,2},{2,4},{4,6},{6,8},{8,10},{10,12},{12,14},{14,16},{16,18},{18... | collective-permute-start | bytes 1572872 | tf_op jit(solution)/shard_map/ppermute | solution.py:17
  15.4 1.2 dynamic-slice
  17.3 0.9 dynamic-update-slice
  18.1 3.1 %all-reduce = s32[64]{0:T(128)S(1)} all-reduce(s32[64]{0:T(128)S(1)} %dynamic-update-slice), channel_id=1, replica_groups=mesh['rows'=16,'cols'=2] {'cols'}, use_global_device_ids=true, to_apply=%add | all-reduce | flops 64 | bytes 512
  21.2 2.3 %collective-permute-start.1 = (s32[64]{0:T(128)S(1)}, s32[64]{0:T(128)S(1)}, u32[]{:S(2)}, u32[]{:S(2)}) collective-permute-start(s32[64]{0:T(128)S(1)} %all-reduce), channel_id=1, source_target_pairs={{2,0},{4,2},{6,4},{8,6},{10,8},{12,10},{14,12},{16,14},{18,16},{20... | collective-permute-start | bytes 776 | tf_op jit(solution)/shard_map/ppermute | solution.py:20
  23.5 3.3 %collective-permute-start = (s32[64]{0:T(128)S(1)}, s32[64]{0:T(128)S(1)}, u32[]{:S(2)}, u32[]{:S(2)}) collective-permute-start(s32[64]{0:T(128)S(1)} %all-reduce), channel_id=1, source_target_pairs={{0,2},{2,4},{4,6},{6,8},{8,10},{10,12},{12,14},{14,16},{16,18},{18... | collective-permute-start | bytes 776 | tf_op jit(solution)/shard_map/ppermute | solution.py:17
  26.8 1.5 reshape.51
  28.3 0.8 reshape.53
  29.1 0.7 add_select_fusion
  29.8 0.7 broadcast_multiply_fusion
  30.5 0.1 reshape.59
  30.6 0.0 copy-start
  30.6 0.0 copy-start.1
  30.6 8.1 %convolution_convert_fusion = bf16[32,64,1728]{2,1,0:T(8,128)(2,1)} fusion(bf16[32,64,64]{2,1,0:T(8,128)(2,1)S(1)} %reshape.51, bf16[32,64,1728]{2,1,0:T(8,128)(2,1)} %param.5), kind=kOutput, calls=%fused_computation.6 | convolution fusion | flops 456523776 | bytes 14417920 | tf_op jit(solution)/shard_map/ips,isn->ipn/dot_general | solution.py:51
  38.8 0.0 copy-done
  38.8 0.0 copy-done.1
  38.8 0.1 fusion.18
  38.9 22.9 %reshape.52 = bf16[32,64,27,64]{3,2,1,0:T(8,128)(2,1)} reshape(bf16[32,64,1728]{2,1,0:T(8,128)(2,1)} %convolution_convert_fusion) | data formatting | bytes 14155776 | tf_op jit(solution)/shard_map/reshape | solution.py:54
  61.8 0.1 copy.10
  61.9 0.0 collective-permute-done.1
  61.9 0.0 collective-permute-done
  61.9 0.1 pad_add_fusion
  62.0 5.8 %gather_fusion = s32[864]{0:T(1024)S(1)} fusion(s32[192]{0:T(256)S(1)} %pad_add_fusion, s32[1024]{0:T(1024)S(1)} %pad_clamp_fusion.1), kind=kCustom, calls=%fused_computation | custom fusion | bytes 10368 | tf_op jit(solution)/shard_map/gather | solution.py:44
  67.7 0.1 reshape.58
  67.8 0.1 fusion.15
  67.9 0.1 copy.9
  68.0 0.0 collective-permute-done.3
  68.0 0.0 collective-permute-done.2
  68.0 0.2 pad_maximum_fusion
  68.2 6.5 %gather_fusion.1 = bf16[864,4096]{1,0:T(8,128)(2,1)} fusion(bf16[192,4096]{1,0:T(8,128)(2,1)S(1)} %pad_maximum_fusion, s32[1024]{0:T(1024)S(1)} %pad_clamp_fusion), kind=kCustom, calls=%fused_computation.1 | custom fusion | bytes 14159232 | tf_op jit(solution)/shard_map/gather | solution.py:55
  74.7 20.0 %reshape.54 = bf16[32,27,64,64]{3,2,1,0:T(8,128)(2,1)} reshape(bf16[864,4096]{1,0:T(8,128)(2,1)} %gather_fusion.1) | data formatting | bytes 14155776 | tf_op jit(solution)/shard_map/reshape | solution.py:55
  94.7 23.6 %fusion.2 = f32[32,27,64,64]{3,2,1,0:T(8,128)} fusion(bf16[32,27,64,64]{3,2,1,0:T(8,128)(2,1)} %reshape.54, bf16[32,64,27,64]{3,2,1,0:T(8,128)(2,1)} %reshape.52), kind=kOutput, calls=%fused_computation.4 | convolution fusion | flops 452984832 | bytes 28311552 | tf_op jit(solution)/shard_map/ipks,ikqs->ikpq/dot_general | solution.py:56
  118.3 41.4 %fusion.4 = f32[24,64,64]{2,0,1:T(8,128)S(1)} fusion(f32[32,27,64,64]{3,2,1,0:T(8,128)} %fusion.2, f32[32,27]{0,1:T(8,128)S(1)} %copy.10, s32[32,27]{0,1:T(8,128)S(1)} %copy.9), kind=kOutput, calls=%fused_computation.8 | convolution fusion | flops 1019257344 | bytes 14555904 | tf_op jit(solution)/shard_map/ikm,ikpq->mpq/dot_general | solution.py:59
  159.7 0.2 copy.11
  159.9 0.5 copy.12
  160.4 1.0 reshape.56
  (4 shorter events, 0.0 us)
Async XLA Ops:
  9.0 59.0 %collective-permute-start.3 = (bf16[64,4096]{1,0:T(8,128)(2,1)S(1)}, bf16[64,4096]{1,0:T(8,128)(2,1)S(1)}, u32[]{:S(2)}, u32[]{:S(2)}) collective-permute-start(bf16[64,4096]{1,0:T(8,128)(2,1)S(1)} %all_gather.7), channel_id=1, source_target_pairs={{2,0},{4,2},{6,4},{8,6},{10,8},{12,10},{14,12},{16,14},{18,16},{20... | collective-permute-start | bytes 1572872 | tf_op jit(solution)/shard_map/ppermute | solution.py:20
  12.2 55.9 %collective-permute-start.2 = (bf16[64,4096]{1,0:T(8,128)(2,1)S(1)}, bf16[64,4096]{1,0:T(8,128)(2,1)S(1)}, u32[]{:S(2)}, u32[]{:S(2)}) collective-permute-start(bf16[64,4096]{1,0:T(8,128)(2,1)S(1)} %all_gather.7), channel_id=1, source_target_pairs={{0,2},{2,4},{4,6},{6,8},{8,10},{10,12},{12,14},{14,16},{16,18},{18... | collective-permute-start | bytes 1572872 | tf_op jit(solution)/shard_map/ppermute | solution.py:17
  21.2 40.6 %collective-permute-start.1 = (s32[64]{0:T(128)S(1)}, s32[64]{0:T(128)S(1)}, u32[]{:S(2)}, u32[]{:S(2)}) collective-permute-start(s32[64]{0:T(128)S(1)} %all-reduce), channel_id=1, source_target_pairs={{2,0},{4,2},{6,4},{8,6},{10,8},{12,10},{14,12},{16,14},{18,16},{20... | collective-permute-start | bytes 776 | tf_op jit(solution)/shard_map/ppermute | solution.py:20
  23.5 38.4 %collective-permute-start = (s32[64]{0:T(128)S(1)}, s32[64]{0:T(128)S(1)}, u32[]{:S(2)}, u32[]{:S(2)}) collective-permute-start(s32[64]{0:T(128)S(1)} %all-reduce), channel_id=1, source_target_pairs={{0,2},{2,4},{4,6},{6,8},{8,10},{10,12},{12,14},{14,16},{16,18},{18... | collective-permute-start | bytes 776 | tf_op jit(solution)/shard_map/ppermute | solution.py:17
  30.6 8.1 %copy-start = (s32[32,27]{1,0:T(8,128)S(1)}, s32[32,27]{1,0:T(8,128)}, u32[]{:S(2)}) copy-start(s32[32,27]{1,0:T(8,128)} %param.7) | copy-start | bytes 10372
  30.6 8.1 %copy-start.1 = (s32[32]{0:T(128)S(1)}, s32[32]{0:T(128)}, u32[]{:S(2)}) copy-start(s32[32]{0:T(128)} %param.8) | copy-start | bytes 388
where the time goes:
time: 163 us; the launch traced here: 161 us
  matrix products  73.2 us (45%)
  local copies, waits for them, and re-layouts  61.6 us (38%)
  blocking collectives  12.1 us (7%)
  starting transfers between devices  11.9 us (7%)
  other arithmetic  1.79 us (1%)
    dot_general x1, matrix products, per_device(): jnp.einsum('ikm,ikpq->mpq', one_hot, products, precision=lax.Precision.HI...  41.4 us
    dot_general x1, matrix products, per_device(): jnp.einsum('ipks,ikqs->ikpq', left_prod, far_blocks, preferred_element_ty...  23.6 us
    reshape x1, local copies, waits for them, and re-layouts, per_device(): left_prod.astype(jnp.bfloat16).reshape(ROWS_DEV, BLK, SLOTS, BLK)  22.9 us
    reshape x1, local copies, waits for them, and re-layouts, per_device(): near_blocks[columns.reshape(-1)].reshape(ROWS_DEV, SLOTS, BLK, BLK)  20 us
    all_gather x1, blocking collectives, per_device(): lax.all_gather(restrict, 'cols', axis=0, tiled=True)  9.02 us
    dot_general x1, matrix products, per_device(): jnp.einsum('ips,isn->ipn', own_blocks, matrix_blocks, preferred_element_t...  8.12 us
    gather x1, local copies, waits for them, and re-layouts, per_device(): near_blocks[columns.reshape(-1)].reshape(ROWS_DEV, SLOTS, BLK, BLK)  6.54 us
    ppermute x2, starting transfers between devices, padded(): lax.ppermute(lax.slice_in_dim(block, block.shape[dim] - width, None, axis...  6.46 us
  transfers between devices with their start and end apart: 4, of which 0 were waited for; matrix products, arithmetic and copies ran while one was open for 27% of the time, Pallas kernels for 0%

commit v1 on v0

v1 whole, which is shorter than its diff:
```python
import functools

import jax
import jax.numpy as jnp
from jax import lax
from jax.experimental import pallas as pl
from jax.experimental.pallas import tpu as pltpu
from jax.sharding import PartitionSpec as P

BLK = 64
SLOTS = 27
ROWS_DEV = 32
AGG_DEV = 2

LANES = 2 * BLK
PAIRS = ROWS_DEV // 2
HALF = PAIRS // 2
TAG = 16
HALF_ROWS = HALF * BLK + TAG
PAYLOAD = 2 * HALF_ROWS
ROW_PAIRS_STEP = 4
CHUNK = 6
MIB = 1 << 20


def pack_kernel(aggregate_ref, restrict_ref, out_ref, wide_ref):
    low = lax.broadcasted_iota(jnp.int32, (PAIRS, LANES), 1) < BLK
    for t in range(BLK // 2):
        x = restrict_ref[:, t * LANES : (t + 1) * LANES].astype(jnp.float32)
        first, second = x[:PAIRS], x[PAIRS:]
        even = jnp.where(low, first, pltpu.roll(second, BLK, 1))
        odd = jnp.where(low, pltpu.roll(first, BLK, 1), second)
        wide_ref[pl.ds(2 * t, PAIRS, stride=BLK), :] = even
        wide_ref[pl.ds(2 * t + 1, PAIRS, stride=BLK), :] = odd
    row = lax.broadcasted_iota(jnp.int32, (TAG, LANES), 0)
    low = lax.broadcasted_iota(jnp.int32, (TAG, LANES), 1) < BLK
    for half in range(2):
        base = half * HALF_ROWS
        out_ref[base : base + HALF * BLK, :] = wide_ref[
            half * HALF * BLK : (half + 1) * HALF * BLK, :
        ].astype(jnp.bfloat16)
        tags = jnp.zeros((TAG, LANES), jnp.int32)
        for p in range(HALF):
            g = half * HALF + p
            tags = jnp.where(
                row == p, jnp.where(low, aggregate_ref[g], aggregate_ref[g + PAIRS]), tags
            )
        out_ref[base + HALF * BLK : base + HALF_ROWS, :] = tags.astype(jnp.float32).astype(
            jnp.bfloat16
        )


def pack(aggregate, restrict):
    return pl.pallas_call(
        pack_kernel,
        out_shape=jax.ShapeDtypeStruct((PAYLOAD, LANES), jnp.bfloat16),
        in_specs=[
            pl.BlockSpec(memory_space=pltpu.SMEM),
            pl.BlockSpec(memory_space=pltpu.VMEM),
        ],
        out_specs=pl.BlockSpec(memory_space=pltpu.VMEM),
        scratch_shapes=[pltpu.VMEM((PAIRS * BLK, LANES), jnp.float32)],
        compiler_params=pltpu.CompilerParams(vmem_limit_bytes=8 * MIB),
        name="pack_payload",
    )(aggregate, restrict)


def left_kernel(order, columns_ref, counts_ref, aggregate_ref, payload_ref, matrix_ref, out_ref, sums_ref):
    chunk, step = pl.program_id(0), pl.program_id(1)
    steps = pl.num_programs(1)
    blocks = out_ref.shape[0]
    width = blocks * ROWS_DEV
    places = order()

    @pl.when(step == 0)
    def _():
        sums_ref[...] = jnp.zeros_like(sums_ref)

    lanes = lax.broadcasted_iota(jnp.int32, (BLK, LANES), 1)
    low, high = lanes < BLK, lanes >= BLK
    base = chunk * width

    def row_pair(local):
        pair = step * ROW_PAIRS_STEP + local
        half = pair // HALF
        start = pl.multiple_of(half * HALF_ROWS + (pair - half * HALF) * BLK, 16)
        both = payload_ref[pl.ds(start, BLK), :]
        zero = jnp.zeros_like(both)
        lhs = jnp.concatenate([jnp.where(low, both, zero), jnp.where(high, both, zero)], axis=0)
        rows = (pair, pair + PAIRS)
        places_of = []
        for row in rows:
            count = counts_ref[row]
            offset = aggregate_ref[row] * width
            places_of.append(
                [
                    jnp.where(
                        (k < count)
                        & (columns_ref[row, k] >= base)
                        & (columns_ref[row, k] < base + width),
                        offset + columns_ref[row, k] - base,
                        AGG_DEV * width,
                    )
                    for k in range(SLOTS)
                ]
            )
        for first in range(0, SLOTS, 4):
            many = min(4, SLOTS - first)
            cut = slice(first * BLK, (first + many) * BLK)
            rhs = jnp.concatenate(
                [matrix_ref[0, local, :, cut], matrix_ref[1, local, :, cut]], axis=0
            )
            left = jnp.dot(lhs, rhs, preferred_element_type=jnp.float32)
            left = left.astype(jnp.bfloat16).astype(jnp.float32)
            for r in range(2):
                for k in range(0, many, 2):
                    x = left[r * BLK : (r + 1) * BLK, k * BLK : min(k + 2, many) * BLK]
                    place = places_of[r][first + k]
                    if k + 1 < many:
                        other = places_of[r][first + k + 1]
                        x_low = sums_ref[place] + x
                        x_high = sums_ref[other] + x
                        pltpu.store(sums_ref.at[place], x_low, mask=low)
                        pltpu.store(sums_ref.at[other], x_high, mask=high)
                    else:
                        sums_ref[place, :, :BLK] = sums_ref[place, :, :BLK] + x

    for local in range(ROW_PAIRS_STEP):
        row_pair(local)

    @pl.when(step == steps - 1)
    def _():
        for position in range(blocks):
            start = (places[position] if places is not None else position) * ROWS_DEV
            for a in range(AGG_DEV):
                for p in range(PAIRS):
                    g = a * width + start + p
                    one, two = sums_ref[g], sums_ref[g + PAIRS]
                    one = one + pltpu.roll(one, BLK, 1)
                    two = two + pltpu.roll(two, BLK, 1)
                    out_ref[position, a * BLK : (a + 1) * BLK, p * LANES : (p + 1) * LANES] = (
                        jnp.where(low, one, two).astype(jnp.bfloat16)
                    )


def left_sums(columns, counts, aggregate, payload, matrix_blocks, total, order):
    blocks = CHUNK if total % CHUNK == 0 else CHUNK // 2
    matrix = matrix_blocks.reshape(2, PAIRS, BLK, SLOTS * BLK)
    steps = PAIRS // ROW_PAIRS_STEP
    smem = pl.BlockSpec(memory_space=pltpu.SMEM)
    return pl.pallas_call(
        functools.partial(left_kernel, order),
        grid=(total // blocks, steps),
        out_shape=jax.ShapeDtypeStruct((total, AGG_DEV * BLK, PAIRS * LANES), jnp.bfloat16),
        in_specs=[
            smem,
            smem,
            smem,
            pl.BlockSpec((PAYLOAD, LANES), lambda c, s: (0, 0)),
            pl.BlockSpec((2, ROW_PAIRS_STEP, BLK, SLOTS * BLK), lambda c, s: (0, s, 0, 0)),
        ],
        out_specs=pl.BlockSpec((blocks, AGG_DEV * BLK, PAIRS * LANES), lambda c, s: (c, 0, 0)),
        scratch_shapes=[
            pltpu.VMEM((AGG_DEV * blocks * ROWS_DEV + 1, BLK, LANES), jnp.float32)
        ],
        compiler_params=pltpu.CompilerParams(vmem_limit_bytes=40 * MIB),
        cost_estimate=pl.CostEstimate(
            flops=2 * ROWS_DEV * SLOTS * BLK**3, bytes_accessed=12 * MIB, transcendentals=0
        ),
        name="left_sums",
    )(columns, counts, aggregate, payload, matrix)


def half_product(lefts, half, piece):
    tags = piece[HALF * BLK : HALF_ROWS, :].astype(jnp.float32)
    masks = [(tags == j).astype(jnp.float32).astype(jnp.bfloat16) for j in range(AGG_DEV)]
    rhs = jnp.concatenate(
        [
            jnp.concatenate(
                [piece[p * BLK : (p + 1) * BLK, :] * masks[j][p : p + 1, :] for p in range(HALF)],
                axis=1,
            )
            for j in range(AGG_DEV)
        ],
        axis=0,
    )
    cut = lefts[:, half * HALF * LANES : (half + 1) * HALF * LANES]
    return lax.dot_general(
        cut, rhs, (((1,), (1,)), ((), ())), preferred_element_type=jnp.float32
    )


def right_kernel(sources, order, first, carried, lefts_ref, *refs):
    out_ref = refs[-1]
    if carried:
        out_ref[...] = refs[-2][...]
    places = order()
    for position, halves in enumerate(sources):
        lefts = lefts_ref[position]
        total = 0.0
        for half, (index, start) in enumerate(halves):
            piece = refs[index][start : start + HALF_ROWS, :]
            total = total + half_product(lefts, half, piece)
        place = places[first + position]
        if not isinstance(place, int):
            place = pl.multiple_of(place * LANES, LANES)
        else:
            place = place * LANES
        for a in range(AGG_DEV):
            out_ref[a, :, pl.ds(place, LANES)] = total[a * BLK : (a + 1) * BLK]


def right_products(lefts, pieces, sources, order, first, width, so_far):
    carried = so_far is not None
    many = len(sources)
    vmem = pl.BlockSpec(memory_space=pltpu.VMEM)
    shape = jax.ShapeDtypeStruct((AGG_DEV, BLK, width), jnp.float32)
    return pl.pallas_call(
        functools.partial(right_kernel, sources, order, first, carried),
        grid=(1,),
        out_shape=shape,
        in_specs=[
            pl.BlockSpec((many,) + lefts.shape[1:], lambda s: (first // many, 0, 0))
        ]
        + [pl.BlockSpec(piece.shape, lambda s: (0, 0)) for piece in pieces]
        + ([pl.BlockSpec(shape.shape, lambda s: (0, 0, 0))] if carried else []),
        out_specs=pl.BlockSpec(shape.shape, lambda s: (0, 0, 0)),
        compiler_params=pltpu.CompilerParams(vmem_limit_bytes=24 * MIB),
        cost_estimate=pl.CostEstimate(
            flops=2 * many * (AGG_DEV * BLK) ** 2 * PAIRS * LANES,
            bytes_accessed=many * 2 * MIB,
            transcendentals=0,
        ),
        name="right_products",
    )(lefts, *pieces, *([so_far] if carried else []))


def paired_plan(columns, counts, aggregate, matrix_blocks, payload, row_count):
    odds = [(i, i + 1) for i in range(1, row_count - 1, 2)]
    odds = odds + [(b, a) for a, b in odds]
    evens = [(i, i ^ 1) for i in range(row_count)]
    across = lambda x: lax.ppermute(x, "cols", [(0, 1), (1, 0)])
    even = lambda x: lax.ppermute(x, "rows", evens)
    odd = lambda x: lax.ppermute(x, "rows", odds)

    def order():
        c, up = lax.axis_index("cols"), 1 - lax.rem(lax.axis_index("rows"), 2)
        near, far = 4 * up, 4 * (1 - up)
        return [2 + c, 3 - c, near + c, near + 1 - c, far + c, far + 1 - c]

    beside = across(payload)
    ahead = odd(payload)
    inner = even(payload)
    inner_beside = even(beside)
    far_first = odd(beside[:HALF_ROWS])
    far_second = across(ahead[HALF_ROWS:])
    lefts = left_sums(columns, counts, aggregate, payload, matrix_blocks, 6, order)
    whole = lambda index: ((index, 0), (index, HALF_ROWS))
    near = right_products(
        lefts,
        [payload, beside, inner, inner_beside],
        [whole(0), whole(1), whole(2), whole(3)],
        order,
        0,
        6 * LANES,
        None,
    )
    return right_products(
        lefts,
        [ahead, far_first, far_second],
        [whole(0), ((1, 0), (2, 0))],
        order,
        4,
        6 * LANES,
        near,
    )


def general_plan(columns, counts, aggregate, matrix_blocks, payload, row_count, col_count):
    forward = [(i, i + 1) for i in range(row_count - 1)]
    backward = [(b, a) for a, b in forward]
    slab = lax.all_gather(payload, "cols", axis=0, tiled=True)
    pieces = [lax.ppermute(slab, "rows", forward), slab, lax.ppermute(slab, "rows", backward)]
    total = 3 * col_count
    order = lambda: list(range(total))
    lefts = left_sums(columns, counts, aggregate, payload, matrix_blocks, total, lambda: None)
    sources = [
        tuple((s, (c * 2 + half) * HALF_ROWS) for half in range(2))
        for s in range(3)
        for c in range(col_count)
    ]
    return right_products(lefts, pieces, sources, order, 0, total * LANES, None)


def per_device(matrix_blocks, restrict, columns, counts, aggregate):
    col_count = lax.axis_size("cols")
    row_count = lax.axis_size("rows")
    payload = pack(aggregate, restrict)
    if col_count == 2 and row_count % 2 == 0:
        return paired_plan(columns, counts, aggregate, matrix_blocks, payload, row_count)
    return general_plan(
        columns, counts, aggregate, matrix_blocks, payload, row_count, col_count
    )


def solution(mesh):
    return jax.shard_map(
        per_device,
        mesh=mesh,
        in_specs=(
            P(("rows", "cols"), None, None),
            P(("rows", "cols"), None),
            P(("rows", "cols"), None),
            P(("rows", "cols")),
            P(("rows", "cols")),
        ),
        out_specs=P(("rows", "cols"), None, None),
        check_vma=False,
    )
```

time: 163 us -> 35 us (0.21)
  matrix products: 73.2 us -> 0 us
  local copies, waits for them, and re-layouts: 61.6 us -> 6.73 us
  Pallas kernels: 0 us -> 13.8 us
  blocking collectives: 12.1 us -> 0 us
  waiting for transfers between devices: 0.01 us -> 2.19 us
  other arithmetic: 1.79 us -> 0 us
    dot_general x3 -> x0, matrix products: 73.2 us -> none  [the longest x1 41.4 us: per_device(): jnp.einsum('ikm,ikpq->mpq', one_hot, products, precision=lax.Precision.HI...]
    reshape x5 -> x0, local copies, waits for them, and re-layouts: 46.2 us -> none  [the longest x1 22.9 us: per_device(): left_prod.astype(jnp.bfloat16).reshape(ROWS_DEV, BLK, SLOTS, BLK)]
    pallas_call x0 -> x4, Pallas kernels: none -> 13.8 us  [the longest x1 10.8 us: left_sums(): pl.pallas_call(functools.partial(left_kernel, order), grid=(total // bloc...]
    gather x3 -> x0, local copies, waits for them, and re-layouts: 12.4 us -> none  [the longest x1 6.54 us: per_device(): near_blocks[columns.reshape(-1)].reshape(ROWS_DEV, SLOTS, BLK, BLK)]
    all_gather x1 -> x0, blocking collectives: 9.02 us -> none  [per_device(): lax.all_gather(restrict, 'cols', axis=0, tiled=True)]
    unnamed x7 -> x12, local copies, waits for them, and re-layouts: 2.11 us -> 6.71 us
    unnamed x1 -> x0, blocking collectives: 3.11 us -> none
    ppermute x4 -> x6, waiting for transfers between devices: 0.01 us -> 2.19 us  [the longest x2 2.18 us: paired_plan(): across = lambda x: lax.ppermute(x, 'cols', [(0, 1), (1, 0)])]
  transfers between devices with their start and end apart: 4 -> 6, of which waited for: 0 -> 1; matrix products, arithmetic and copies ran while one was open for 27% -> 0% of each run, Pallas kernels for 0% -> 33%
where the time goes in v1:
time: 35 us; the launch traced here: 34.7 us
  Pallas kernels  13.8 us (39%)
  starting transfers between devices  11.9 us (34%)
  local copies, waits for them, and re-layouts  6.73 us (19%)
  waiting for transfers between devices  2.19 us (6%)
    pallas_call x1, Pallas kernels, left_sums(): pl.pallas_call(functools.partial(left_kernel, order), grid=(total // bloc...  10.8 us
    ppermute x2, starting transfers between devices, paired_plan(): odd = lambda x: lax.ppermute(x, 'rows', odds)  7.18 us
    unnamed x12, local copies, waits for them, and re-layouts  6.71 us
    ppermute x2, starting transfers between devices, paired_plan(): across = lambda x: lax.ppermute(x, 'cols', [(0, 1), (1, 0)])  3.44 us
    ppermute x2, waiting for transfers between devices, paired_plan(): across = lambda x: lax.ppermute(x, 'cols', [(0, 1), (1, 0)])  2.18 us
    pallas_call x2, Pallas kernels, right_products(): pl.pallas_call(functools.partial(right_kernel, sources, order, first, car...  1.93 us
    ppermute x2, starting transfers between devices, paired_plan(): even = lambda x: lax.ppermute(x, 'rows', evens)  1.3 us
    pallas_call x1, Pallas kernels, pack(): pl.pallas_call(pack_kernel, out_shape=jax.ShapeDtypeStruct((PAYLOAD, LANE...  1.06 us
  transfers between devices with their start and end apart: 6, of which 1 were waited for; matrix products, arithmetic and copies ran while one was open for 0% of the time, Pallas kernels for 33%

profile of v1, /device:TPU:1, one launch (start us, length us, event | category | flops | bytes accessed | tf_op | source)
XLA Modules:
  0.0 34.7 jit_solution(2276104300335379904)
XLA Ops:
  0.0 0.0 copy-start.1
  0.0 0.9 %copy-done.1 = bf16[32,4096]{1,0:T(8,128)(2,1)S(1)} copy-done((bf16[32,4096]{1,0:T(8,128)(2,1)S(1)}, bf16[32,4096]{1,0:T(8,128)(2,1)}, u32[]{:S(2)}) %copy-start.1) | copy-done | bytes 262168
  1.0 0.0 copy-start.3
  1.0 0.7 %copy-done.3 = s32[32]{0:T(128)S(1)} copy-done((s32[32]{0:T(128)S(1)}, s32[32]{0:T(128)}, u32[]{:S(2)}) %copy-start.3) | copy-done | bytes 152
  1.6 1.1 %pack_payload.1.payload_ref.refs_0_ = bf16[1056,128]{1,0:T(8,128)(2,1)S(1)} custom-call(s32[32]{0:T(128)S(1)} %copy-done.3, bf16[32,4096]{1,0:T(8,128)(2,1)S(1)} %copy-done.1), custom_call_target="tpu_custom_call" | custom-call | tf_op jit(solution)/shard_map/pack_payload/pallas_call | solution.py:54
  2.7 2.1 %collective-permute-start.1 = (bf16[1056,128]{1,0:T(8,128)(2,1)S(1)}, bf16[1056,128]{1,0:T(8,128)(2,1)S(1)}, u32[]{:S(2)}, u32[]{:S(2)}) collective-permute-start(bf16[1056,128]{1,0:T(8,128)(2,1)S(1)} %pack_payload.1.payload_ref.refs_0_), channel_id=1, source_target_pairs={{0,1},{1,0},{2,3},{3,2},{4,5},{5,4},{6,7},{7,6},{8,9},{9,8},{10,11... | collective-permute-start | bytes 811016 | tf_op jit(solution)/shard_map/ppermute | solution.py:242
  4.8 3.9 %collective-permute-start = (bf16[1056,128]{1,0:T(8,128)(2,1)S(1)}, bf16[1056,128]{1,0:T(8,128)(2,1)S(1)}, u32[]{:S(2)}, u32[]{:S(2)}) collective-permute-start(bf16[1056,128]{1,0:T(8,128)(2,1)S(1)} %pack_payload.1.payload_ref.refs_0_), channel_id=1, source_target_pairs={{2,4},{6,8},{10,12},{14,16},{18,20},{22,24},{26,28},{4,2},{8,6},{1... | collective-permute-start | bytes 811016 | tf_op jit(solution)/shard_map/ppermute | solution.py:244
  8.8 0.1 collective-permute-start.4
  8.8 2.2 %collective-permute-done.1.refs_1_ = bf16[1056,128]{1,0:T(8,128)(2,1)S(1)} collective-permute-done((bf16[1056,128]{1,0:T(8,128)(2,1)S(1)}, bf16[1056,128]{1,0:T(8,128)(2,1)S(1)}, u32[]{:S(2)}, u32[]{:S(2)}) %collective-permute-start.1) | collective-permute-done | bytes 270368 | tf_op jit(solution)/shard_map/ppermute | solution.py:242
  11.0 1.2 %collective-permute-start.5 = (bf16[1056,128]{1,0:T(8,128)(2,1)S(1)}, bf16[1056,128]{1,0:T(8,128)(2,1)S(1)}, u32[]{:S(2)}, u32[]{:S(2)}) collective-permute-start(bf16[1056,128]{1,0:T(8,128)(2,1)S(1)} %collective-permute-done.1.refs_1_), channel_id=1, source_target_pairs={{0,2},{2,0},{4,6},{6,4},{8,10},{10,8},{12,14},{14,12},{16,18},{18,... | collective-permute-start | bytes 811016 | tf_op jit(solution)/shard_map/ppermute | solution.py:243
  12.3 3.2 %collective-permute-start.2 = (bf16[528,128]{1,0:T(8,128)(2,1)S(1)}, bf16[528,128]{1,0:T(8,128)(2,1)S(1)}, u32[]{:S(2)}, u32[]{:S(2)}) collective-permute-start(bf16[528,128]{1,0:T(8,128)(2,1)S(1)} %slice.8), channel_id=1, source_target_pairs={{2,4},{6,8},{10,12},{14,16},{18,20},{22,24},{26,28},{4,2},{8,6},{1... | collective-permute-start | bytes 405512 | tf_op jit(solution)/shard_map/ppermute | solution.py:244
  15.5 0.0 collective-permute-done.refs_0_
  15.5 1.3 %collective-permute-start.3 = (bf16[528,128]{1,0:T(8,128)(2,1)S(1)}, bf16[528,128]{1,0:T(8,128)(2,1)S(1)}, u32[]{:S(2)}, u32[]{:S(2)}) collective-permute-start(bf16[528,128]{1,0:T(8,128)(2,1)S(1)} %slice.9), channel_id=1, source_target_pairs={{0,1},{1,0},{2,3},{3,2},{4,5},{5,4},{6,7},{7,6},{8,9},{9,8},{10,11... | collective-permute-start | bytes 405512 | tf_op jit(solution)/shard_map/ppermute | solution.py:242
  16.8 0.0 copy-start
  16.8 3.1 %copy-done = bf16[32,64,1728]{2,1,0:T(8,128)(2,1)S(1)} copy-done((bf16[32,64,1728]{2,1,0:T(8,128)(2,1)S(1)}, bf16[32,64,1728]{2,1,0:T(8,128)(2,1)}, u32[]{:S(2)}) %copy-start) | copy-done | bytes 7077912
  19.9 0.0 copy-start.2
  19.9 0.7 %copy-done.2 = s32[32,27]{1,0:T(8,128)S(1)} copy-done((s32[32,27]{1,0:T(8,128)S(1)}, s32[32,27]{1,0:T(8,128)}, u32[]{:S(2)}) %copy-start.2) | copy-done | bytes 3480
  20.6 0.0 copy-start.4
  20.6 0.7 %copy-done.4 = s32[32]{0:T(128)S(1)} copy-done((s32[32]{0:T(128)S(1)}, s32[32]{0:T(128)}, u32[]{:S(2)}) %copy-start.4) | copy-done | bytes 152
  21.3 0.0 copy-start.5
  21.3 0.7 %copy-done.5 = s32[32]{0:T(128)S(1)} copy-done((s32[32]{0:T(128)S(1)}, s32[32]{0:T(128)}, u32[]{:S(2)}) %copy-start.5) | copy-done | bytes 152
  21.9 10.8 %left_sums.1.lefts_ref = bf16[6,128,2048]{2,1,0:T(8,128)(2,1)S(1)} custom-call(s32[32,27]{1,0:T(8,128)S(1)} %copy-done.2, s32[32]{0:T(128)S(1)} %copy-done.5, s32[32]{0:T(128)S(1)} %copy-done.4, bf16[1056,128]{1,0:T(8,128)(2,1)S(1)} %pack_payload.1.payload_ref.refs_0_, bf16[2,16,64,1728]{3,2,1,0:T(8,128)(2,1)S(1)} %bitcast.1), custom_call_target="tpu_custom_call" | custom-call | flops 452984832 | bytes 12582912 | tf_op jit(solution)/shard_map/left_sums/pallas_call | solution.py:151
  32.7 0.0 collective-permute-done.4.refs_2_
  32.8 0.0 collective-permute-done.5.refs_3_
  32.8 0.7 %right_products.2.refs_3_ = f32[2,64,768]{2,1,0:T(8,128)S(1)} custom-call(bf16[6,128,2048]{2,1,0:T(8,128)(2,1)S(1)} %left_sums.1.lefts_ref, bf16[1056,128]{1,0:T(8,128)(2,1)S(1)} %pack_payload.1.payload_ref.refs_0_, bf16[1056,128]{1,0:T(8,128)(2,1)S(1)} %collective-permute-done.1.refs_1_, bf16[1056,128]{1,0:T(8,128)(2,1)S(1)} %collective-permute-done.4.refs_2_, ...), custom_call_target="tpu_custom_call" | custom-call | flops 268435456 | bytes 8388608 | tf_op jit(solution)/shard_map/right_products/pallas_call | solution.py:218
  33.5 0.0 collective-permute-done.2.refs_1_
  33.5 0.0 collective-permute-done.3.refs_2_
  33.5 1.2 %right_products.3 = f32[2,64,768]{2,1,0:T(8,128)} custom-call(bf16[6,128,2048]{2,1,0:T(8,128)(2,1)S(1)} %left_sums.1.lefts_ref, bf16[1056,128]{1,0:T(8,128)(2,1)S(1)} %collective-permute-done.refs_0_, bf16[528,128]{1,0:T(8,128)(2,1)S(1)} %collective-permute-done.2.refs_1_, bf16[528,128]{1,0:T(8,128)(2,1)S(1)} %collective-permute-done.3.refs_2_, ...), custom_call_target="tpu_custom_call" | custom-call | flops 134217728 | bytes 4194304 | tf_op jit(solution)/shard_map/right_products/pallas_call | solution.py:218
  (2 shorter events, 0.0 us)
Async XLA Ops:
  0.0 0.9 %copy-start.1 = (bf16[32,4096]{1,0:T(8,128)(2,1)S(1)}, bf16[32,4096]{1,0:T(8,128)(2,1)}, u32[]{:S(2)}) copy-start(bf16[32,4096]{1,0:T(8,128)(2,1)} %restrict_ref.1) | copy-start | bytes 786436
  1.0 0.7 %copy-start.3 = (s32[32]{0:T(128)S(1)}, s32[32]{0:T(128)}, u32[]{:S(2)}) copy-start(s32[32]{0:T(128)} %aggregate_ref.3) | copy-start | bytes 388
  2.7 8.3 %collective-permute-start.1 = (bf16[1056,128]{1,0:T(8,128)(2,1)S(1)}, bf16[1056,128]{1,0:T(8,128)(2,1)S(1)}, u32[]{:S(2)}, u32[]{:S(2)}) collective-permute-start(bf16[1056,128]{1,0:T(8,128)(2,1)S(1)} %pack_payload.1.payload_ref.refs_0_), channel_id=1, source_target_pairs={{0,1},{1,0},{2,3},{3,2},{4,5},{5,4},{6,7},{7,6},{8,9},{9,8},{10,11... | collective-permute-start | bytes 811016 | tf_op jit(solution)/shard_map/ppermute | solution.py:242
  4.8 10.7 %collective-permute-start = (bf16[1056,128]{1,0:T(8,128)(2,1)S(1)}, bf16[1056,128]{1,0:T(8,128)(2,1)S(1)}, u32[]{:S(2)}, u32[]{:S(2)}) collective-permute-start(bf16[1056,128]{1,0:T(8,128)(2,1)S(1)} %pack_payload.1.payload_ref.refs_0_), channel_id=1, source_target_pairs={{2,4},{6,8},{10,12},{14,16},{18,20},{22,24},{26,28},{4,2},{8,6},{1... | collective-permute-start | bytes 811016 | tf_op jit(solution)/shard_map/ppermute | solution.py:244
  8.8 24.0 %collective-permute-start.4 = (bf16[1056,128]{1,0:T(8,128)(2,1)S(1)}, bf16[1056,128]{1,0:T(8,128)(2,1)S(1)}, u32[]{:S(2)}, u32[]{:S(2)}) collective-permute-start(bf16[1056,128]{1,0:T(8,128)(2,1)S(1)} %pack_payload.1.payload_ref.refs_0_), channel_id=1, source_target_pairs={{0,2},{2,0},{4,6},{6,4},{8,10},{10,8},{12,14},{14,12},{16,18},{18,... | collective-permute-start | bytes 811016 | tf_op jit(solution)/shard_map/ppermute | solution.py:243
  11.0 21.7 %collective-permute-start.5 = (bf16[1056,128]{1,0:T(8,128)(2,1)S(1)}, bf16[1056,128]{1,0:T(8,128)(2,1)S(1)}, u32[]{:S(2)}, u32[]{:S(2)}) collective-permute-start(bf16[1056,128]{1,0:T(8,128)(2,1)S(1)} %collective-permute-done.1.refs_1_), channel_id=1, source_target_pairs={{0,2},{2,0},{4,6},{6,4},{8,10},{10,8},{12,14},{14,12},{16,18},{18,... | collective-permute-start | bytes 811016 | tf_op jit(solution)/shard_map/ppermute | solution.py:243
  12.3 21.2 %collective-permute-start.2 = (bf16[528,128]{1,0:T(8,128)(2,1)S(1)}, bf16[528,128]{1,0:T(8,128)(2,1)S(1)}, u32[]{:S(2)}, u32[]{:S(2)}) collective-permute-start(bf16[528,128]{1,0:T(8,128)(2,1)S(1)} %slice.8), channel_id=1, source_target_pairs={{2,4},{6,8},{10,12},{14,16},{18,20},{22,24},{26,28},{4,2},{8,6},{1... | collective-permute-start | bytes 405512 | tf_op jit(solution)/shard_map/ppermute | solution.py:244
  15.5 18.0 %collective-permute-start.3 = (bf16[528,128]{1,0:T(8,128)(2,1)S(1)}, bf16[528,128]{1,0:T(8,128)(2,1)S(1)}, u32[]{:S(2)}, u32[]{:S(2)}) collective-permute-start(bf16[528,128]{1,0:T(8,128)(2,1)S(1)} %slice.9), channel_id=1, source_target_pairs={{0,1},{1,0},{2,3},{3,2},{4,5},{5,4},{6,7},{7,6},{8,9},{9,8},{10,11... | collective-permute-start | bytes 405512 | tf_op jit(solution)/shard_map/ppermute | solution.py:242
  16.8 3.1 %copy-start = (bf16[32,64,1728]{2,1,0:T(8,128)(2,1)S(1)}, bf16[32,64,1728]{2,1,0:T(8,128)(2,1)}, u32[]{:S(2)}) copy-start(bf16[32,64,1728]{2,1,0:T(8,128)(2,1)} %param.5) | copy-start | bytes 21233668
  19.9 0.7 %copy-start.2 = (s32[32,27]{1,0:T(8,128)S(1)}, s32[32,27]{1,0:T(8,128)}, u32[]{:S(2)}) copy-start(s32[32,27]{1,0:T(8,128)} %columns_ref.1) | copy-start | bytes 10372
  20.6 0.7 %copy-start.4 = (s32[32]{0:T(128)S(1)}, s32[32]{0:T(128)}, u32[]{:S(2)}) copy-start(s32[32]{0:T(128)} %aggregate_ref.3) | copy-start | bytes 388
  21.3 0.7 %copy-start.5 = (s32[32]{0:T(128)S(1)}, s32[32]{0:T(128)}, u32[]{:S(2)}) copy-start(s32[32]{0:T(128)} %counts_ref.1) | copy-start | bytes 388

commit v2 on v1

v2 whole, which is shorter than its diff:
```python
import functools

import jax
import jax.numpy as jnp
from jax import lax
from jax.experimental import pallas as pl
from jax.experimental.pallas import tpu as pltpu
from jax.sharding import PartitionSpec as P

BLK = 64
SLOTS = 27
ROWS_DEV = 32
AGG_DEV = 2

LANES = 2 * BLK
PAIRS = ROWS_DEV // 2
HALF = PAIRS // 2
TAG = 16
HALF_ROWS = HALF * BLK + TAG
PAYLOAD = 2 * HALF_ROWS
STEP = 4
DEPTH = 2
CHUNK = 6
MIB = 1 << 20


def pack_kernel(aggregate_hbm, restrict_hbm, out_ref, restrict_ref, wide_ref, aggregate_ref, sems):
    rows = pltpu.make_async_copy(restrict_hbm, restrict_ref, sems.at[0])
    tags = pltpu.make_async_copy(aggregate_hbm, aggregate_ref, sems.at[1])
    rows.start()
    tags.start()
    tags.wait()
    row = lax.broadcasted_iota(jnp.int32, (TAG, LANES), 0)
    low = lax.broadcasted_iota(jnp.int32, (TAG, LANES), 1) < BLK
    for half in range(2):
        owners = jnp.zeros((TAG, LANES), jnp.int32)
        for p in range(HALF):
            g = half * HALF + p
            owners = jnp.where(
                row == p, jnp.where(low, aggregate_ref[g], aggregate_ref[g + PAIRS]), owners
            )
        last = (half + 1) * HALF_ROWS
        out_ref[last - TAG : last, :] = owners.astype(jnp.float32).astype(jnp.bfloat16)
    rows.wait()
    low = lax.broadcasted_iota(jnp.int32, (PAIRS, LANES), 1) < BLK
    for t in range(BLK // 2):
        x = restrict_ref[:, t * LANES : (t + 1) * LANES].astype(jnp.float32)
        first, second = x[:PAIRS], x[PAIRS:]
        even = jnp.where(low, first, pltpu.roll(second, BLK, 1))
        odd = jnp.where(low, pltpu.roll(first, BLK, 1), second)
        wide_ref[pl.ds(2 * t, PAIRS, stride=BLK), :] = even
        wide_ref[pl.ds(2 * t + 1, PAIRS, stride=BLK), :] = odd
    for half in range(2):
        out_ref[half * HALF_ROWS : half * HALF_ROWS + HALF * BLK, :] = wide_ref[
            half * HALF * BLK : (half + 1) * HALF * BLK, :
        ].astype(jnp.bfloat16)


def pack(aggregate, restrict):
    hbm = pl.BlockSpec(memory_space=pltpu.HBM)
    return pl.pallas_call(
        pack_kernel,
        out_shape=jax.ShapeDtypeStruct((PAYLOAD, LANES), jnp.bfloat16),
        in_specs=[hbm, hbm],
        out_specs=pl.BlockSpec(memory_space=pltpu.VMEM),
        scratch_shapes=[
            pltpu.VMEM(restrict.shape, restrict.dtype),
            pltpu.VMEM((PAIRS * BLK, LANES), jnp.float32),
            pltpu.SMEM(aggregate.shape, aggregate.dtype),
            pltpu.SemaphoreType.DMA((2,)),
        ],
        compiler_params=pltpu.CompilerParams(vmem_limit_bytes=8 * MIB),
        name="pack_payload",
    )(*(pltpu.with_memory_space_constraint(x, pltpu.HBM) for x in (aggregate, restrict)))


def left_kernel(
    order,
    columns_hbm,
    counts_hbm,
    aggregate_hbm,
    payload_ref,
    matrix_hbm,
    out_ref,
    matrix_ref,
    sums_ref,
    columns_ref,
    counts_ref,
    aggregate_ref,
    matrix_sems,
    sems,
):
    total = out_ref.shape[0]
    blocks = CHUNK if total % CHUNK == 0 else CHUNK // 2
    width = blocks * ROWS_DEV
    places = order()
    short = BLK // 2
    steps = PAIRS // STEP

    def rows_copy(step):
        cut = pl.ds(step * STEP, STEP)
        return pltpu.make_async_copy(
            matrix_hbm.at[:, cut], matrix_ref.at[:, cut], matrix_sems.at[step]
        )

    small = [
        pltpu.make_async_copy(columns_hbm, columns_ref, sems.at[0]),
        pltpu.make_async_copy(counts_hbm, counts_ref, sems.at[1]),
        pltpu.make_async_copy(aggregate_hbm, aggregate_ref, sems.at[2]),
    ]
    for copy in small:
        copy.start()
    for step in range(steps):
        rows_copy(step).start()
    low = lax.broadcasted_iota(jnp.int32, (BLK, LANES), 1) < BLK
    low_short = lax.broadcasted_iota(jnp.int32, (short, LANES), 1) < BLK

    def add_all(entries):
        waiting = []
        for place, tile in entries:
            value = sums_ref[place]
            for earlier, earlier_value in waiting:
                value = jnp.where(place == earlier, earlier_value, value)
            value = value + tile
            if len(waiting) == DEPTH:
                sums_ref[waiting[0][0]] = waiting[0][1]
                waiting = waiting[1:]
            waiting = waiting + [(place, value)]
        for place, value in waiting:
            sums_ref[place] = value

    def tiles_of(base, pair):
        half = pair // HALF
        start = pl.multiple_of(half * HALF_ROWS + (pair - half * HALF) * BLK, 16)
        both = payload_ref[pl.ds(start, BLK), :]
        zero = jnp.zeros_like(both)
        lhs = jnp.concatenate([jnp.where(low, both, zero), jnp.where(low, zero, both)], axis=0)
        rows = (pair, pair + PAIRS)
        count = [counts_ref[row] for row in rows]
        offset = [aggregate_ref[row] * width for row in rows]

        def place_of(r, k):
            local = columns_ref[rows[r], k]
            live = k < count[r]
            if total > blocks:
                local = local - base
                live = live & (local >= 0) & (local < width)
            return jnp.where(live, offset[r] + local, AGG_DEV * width)

        for first in range(0, SLOTS, 4):
            many = min(4, SLOTS - first)
            cut = slice(first * BLK, (first + many) * BLK)
            rhs = jnp.concatenate(
                [matrix_ref[0, pair, :, cut], matrix_ref[1, pair, :, cut]], axis=0
            )
            if many * BLK % LANES:
                rhs = jnp.concatenate([rhs, rhs[:, -BLK:]], axis=1)
            left = jnp.dot(lhs, rhs, preferred_element_type=jnp.float32).astype(jnp.bfloat16)
            for k in range(0, many, 2):
                for r in range(2):
                    lanes = slice(k * BLK, (k + 2) * BLK)
                    upper = left[r * BLK : r * BLK + short, lanes]
                    lower = left[r * BLK + short : (r + 1) * BLK, lanes]
                    one = jnp.where(low_short, upper, pltpu.roll(lower, BLK, 1))
                    yield place_of(r, first + k), one.astype(jnp.float32)
                    if k + 1 < many:
                        two = jnp.where(low_short, pltpu.roll(upper, BLK, 1), lower)
                        yield place_of(r, first + k + 1), two.astype(jnp.float32)

    def one_chunk(chunk, first_chunk):
        base = chunk * width
        sums_ref[...] = jnp.zeros_like(sums_ref)
        if first_chunk:
            for copy in small:
                copy.wait()

        def one_step(step, carry):
            if first_chunk:
                rows_copy(step).wait()
            add_all(
                entry for local in range(STEP) for entry in tiles_of(base, step * STEP + local)
            )
            return carry

        lax.fori_loop(0, steps, one_step, 0)
        for position in range(blocks):
            spot, live = places[position] if places is not None else (position, None)
            start = spot * ROWS_DEV
            for a in range(AGG_DEV):
                for p in range(PAIRS):
                    g = a * width + start + p
                    one, two = sums_ref[g], sums_ref[g + PAIRS]
                    if live is not None:
                        one, two = jnp.where(live, one, 0.0), jnp.where(live, two, 0.0)
                    one, two = one.astype(jnp.bfloat16), two.astype(jnp.bfloat16)
                    lanes = slice(p * LANES, (p + 1) * LANES)
                    out_ref[chunk * blocks + position, a * BLK : a * BLK + short, lanes] = (
                        jnp.where(low_short, one, pltpu.roll(two, BLK, 1))
                    )
                    out_ref[
                        chunk * blocks + position, a * BLK + short : (a + 1) * BLK, lanes
                    ] = jnp.where(low_short, pltpu.roll(one, BLK, 1), two)

    one_chunk(0, True)
    if total > blocks:

        def later(chunk, carry):
            one_chunk(chunk, False)
            return carry

        lax.fori_loop(1, total // blocks, later, 0)


def left_sums(columns, counts, aggregate, payload, matrix_blocks, total, order):
    blocks = CHUNK if total % CHUNK == 0 else CHUNK // 2
    matrix = matrix_blocks.reshape(2, PAIRS, BLK, SLOTS * BLK)
    hbm = pl.BlockSpec(memory_space=pltpu.HBM)
    vmem = pl.BlockSpec(memory_space=pltpu.VMEM)
    return pl.pallas_call(
        functools.partial(left_kernel, order),
        out_shape=jax.ShapeDtypeStruct((total, AGG_DEV * BLK, PAIRS * LANES), jnp.bfloat16),
        in_specs=[hbm, hbm, hbm, vmem, hbm],
        out_specs=vmem,
        scratch_shapes=[
            pltpu.VMEM(matrix.shape, matrix.dtype),
            pltpu.VMEM((AGG_DEV * blocks * ROWS_DEV + 1, BLK // 2, LANES), jnp.float32),
            pltpu.SMEM(columns.shape, columns.dtype),
            pltpu.SMEM(counts.shape, counts.dtype),
            pltpu.SMEM(aggregate.shape, aggregate.dtype),
            pltpu.SemaphoreType.DMA((PAIRS // STEP,)),
            pltpu.SemaphoreType.DMA((3,)),
        ],
        compiler_params=pltpu.CompilerParams(vmem_limit_bytes=20 * MIB),
        cost_estimate=pl.CostEstimate(
            flops=40 * ROWS_DEV * SLOTS * BLK**3, bytes_accessed=12 * MIB, transcendentals=0
        ),
        name="left_sums",
    )(
        *(pltpu.with_memory_space_constraint(x, pltpu.HBM) for x in (columns, counts, aggregate)),
        payload,
        pltpu.with_memory_space_constraint(matrix, pltpu.HBM),
    )


def half_product(lefts, half, piece):
    tags = piece[HALF * BLK : HALF_ROWS, :].astype(jnp.float32)
    masks = [(tags == j).astype(jnp.float32).astype(jnp.bfloat16) for j in range(AGG_DEV)]
    rhs = jnp.concatenate(
        [
            jnp.concatenate(
                [piece[p * BLK : (p + 1) * BLK, :] * masks[j][p : p + 1, :] for p in range(HALF)],
                axis=1,
            )
            for j in range(AGG_DEV)
        ],
        axis=0,
    )
    cut = lefts[:, half * HALF * LANES : (half + 1) * HALF * LANES]
    return lax.dot_general(
        cut, rhs, (((1,), (1,)), ((), ())), preferred_element_type=jnp.float32
    )


def right_kernel(sources, order, first, carried, lefts_ref, *refs):
    out_ref = refs[-1]
    if carried:
        out_ref[...] = refs[-2][...]
    places = order()
    for position, halves in enumerate(sources):
        lefts = lefts_ref[first + position]
        total = 0.0
        for half, (index, start) in enumerate(halves):
            piece = refs[index][start : start + HALF_ROWS, :]
            total = total + half_product(lefts, half, piece)
        place, _ = places[first + position]
        if not isinstance(place, int):
            place = pl.multiple_of(place * LANES, LANES)
        else:
            place = place * LANES
        for a in range(AGG_DEV):
            out_ref[a, :, pl.ds(place, LANES)] = total[a * BLK : (a + 1) * BLK]


def right_products(lefts, pieces, sources, order, first, width, so_far, last):
    carried = so_far is not None
    many = len(sources)
    vmem = pl.BlockSpec(memory_space=pltpu.VMEM)
    shape = jax.ShapeDtypeStruct((AGG_DEV, BLK, width), jnp.float32)
    return pl.pallas_call(
        functools.partial(right_kernel, sources, order, first, carried),
        grid=(1,),
        out_shape=shape,
        in_specs=[vmem] * (1 + len(pieces) + carried),
        out_specs=pl.BlockSpec(shape.shape, lambda s: (0, 0, 0)) if last else vmem,
        compiler_params=pltpu.CompilerParams(vmem_limit_bytes=8 * MIB),
        cost_estimate=pl.CostEstimate(
            flops=2 * many * (AGG_DEV * BLK) ** 2 * PAIRS * LANES,
            bytes_accessed=many * MIB // 16,
            transcendentals=0,
        ),
        name="right_products",
    )(lefts, *pieces, *([so_far] if carried else []))


def paired_plan(columns, counts, aggregate, matrix_blocks, payload, row_count):
    ring = [(i, (i + 1) % row_count) for i in range(row_count)]
    across = [(0, 1), (1, 0)]
    evens = [(i, i ^ 1) for i in range(row_count)]
    odds = [(i, i + 1) for i in range(1, row_count - 1, 2)]
    odds = odds + [(b, a) for a, b in odds] + [(0, 0), (row_count - 1, row_count - 1)]
    crossed = [(2 * a + c, 2 * b + 1 - c) for a, b in odds for c in range(2)]

    def order():
        c, row = lax.axis_index("cols"), lax.axis_index("rows")
        up = 1 - lax.rem(row, 2)
        inside = [row > 0, None, row < row_count - 1]
        spots = [(1, c), (1, 1 - c), (0, c), (2, c), (2 * up, 1 - c), (2 - 2 * up, 1 - c)]
        far = (up == 0) & (row < row_count - 1) | (up == 1) & (row > 0)
        return [(2 * slab + col, live) for (slab, col), live in zip(spots, [None, None, inside[0], inside[2], None, far])]

    far = lax.ppermute(payload, ("rows", "cols"), crossed)
    below = lax.ppermute(payload, "rows", ring)
    above = lax.ppermute(payload, "rows", [(b, a) for a, b in ring])
    beside = lax.ppermute(payload, "cols", across)
    lefts = left_sums(columns, counts, aggregate, payload, matrix_blocks, 6, order)
    lefts, beside = lax.optimization_barrier((lefts, beside))
    inner = lax.ppermute(beside, "rows", evens)
    whole = lambda index: ((index, 0), (index, HALF_ROWS))
    return right_products(
        lefts,
        [payload, beside, below, above, inner, far],
        [whole(index) for index in range(6)],
        order,
        0,
        6 * LANES,
        None,
        True,
    )


def general_plan(columns, counts, aggregate, matrix_blocks, payload, row_count, col_count):
    forward = [(i, i + 1) for i in range(row_count - 1)]
    backward = [(b, a) for a, b in forward]
    slab = lax.all_gather(payload, "cols", axis=0, tiled=True)
    pieces = [lax.ppermute(slab, "rows", forward), slab, lax.ppermute(slab, "rows", backward)]
    total = 3 * col_count
    order = lambda: [(block, None) for block in range(total)]
    lefts = left_sums(columns, counts, aggregate, payload, matrix_blocks, total, lambda: None)
    sources = [
        tuple((s, (c * 2 + half) * HALF_ROWS) for half in range(2))
        for s in range(3)
        for c in range(col_count)
    ]
    return right_products(lefts, pieces, sources, order, 0, total * LANES, None, True)


def per_device(matrix_blocks, restrict, columns, counts, aggregate):
    col_count = lax.axis_size("cols")
    row_count = lax.axis_size("rows")
    payload = pack(aggregate, restrict)
    if col_count == 2 and row_count % 2 == 0:
        return paired_plan(columns, counts, aggregate, matrix_blocks, payload, row_count)
    return general_plan(
        columns, counts, aggregate, matrix_blocks, payload, row_count, col_count
    )


def solution(mesh):
    return jax.shard_map(
        per_device,
        mesh=mesh,
        in_specs=(
            P(("rows", "cols"), None, None),
            P(("rows", "cols"), None),
            P(("rows", "cols"), None),
            P(("rows", "cols")),
            P(("rows", "cols")),
        ),
        out_specs=P(("rows", "cols"), None, None),
        check_vma=False,
    )
```

time: 35 us -> 21.1 us (0.60)
  the two profiles are of different devices: /device:TPU:1 before, /device:TPU:0 now
where the time goes in v2:
time: 21.1 us; the launch traced here: 21 us
  Pallas kernels  11.6 us (55%)
  starting transfers between devices  7.23 us (34%)
  waiting for transfers between devices  2.06 us (10%)
    pallas_call x1, Pallas kernels, left_sums(): pl.pallas_call(functools.partial(left_kernel, order), out_shape=jax.Shape...  8.39 us
    ppermute x1, starting transfers between devices, paired_plan(): above = lax.ppermute(payload, 'rows', [(b, a) for a, b in ring])  3.69 us
    ppermute x1, starting transfers between devices, paired_plan(): far = lax.ppermute(payload, ('rows', 'cols'), crossed)  3.03 us
    pallas_call x1, Pallas kernels, right_products(): pl.pallas_call(functools.partial(right_kernel, sources, order, first, car...  1.76 us
    ppermute x1, waiting for transfers between devices, paired_plan(): inner = lax.ppermute(beside, 'rows', evens)  1.52 us
    pallas_call x1, Pallas kernels, pack(): pl.pallas_call(pack_kernel, out_shape=jax.ShapeDtypeStruct((PAYLOAD, LANE...  1.5 us
    ppermute x1, waiting for transfers between devices, paired_plan(): beside = lax.ppermute(payload, 'cols', across)  0.53 us
    ppermute x1, starting transfers between devices, paired_plan(): beside = lax.ppermute(payload, 'cols', across)  0.51 us
  transfers between devices with their start and end apart: 5, of which 2 were waited for; matrix products, arithmetic and copies ran while one was open for 0% of the time, Pallas kernels for 40%

profile of v2, /device:TPU:0, one launch (start us, length us, event | category | flops | bytes accessed | tf_op | source)
XLA Modules:
  0.0 21.0 jit_solution(7642467550457745127)
XLA Ops:
  0.0 1.5 %pack_payload.1.payload_ref.refs_0_ = bf16[1056,128]{1,0:T(8,128)(2,1)S(1)} custom-call(s32[32]{0:T(128)} %aggregate_hbm.3, bf16[32,4096]{1,0:T(8,128)(2,1)} %restrict_hbm.1), custom_call_target="tpu_custom_call" | custom-call | tf_op jit(solution)/shard_map/pack_payload/pallas_call | solution.py:61
  1.5 3.0 %collective-permute-start.4 = (bf16[1056,128]{1,0:T(8,128)(2,1)S(1)}, bf16[1056,128]{1,0:T(8,128)(2,1)S(1)}, u32[]{:S(2)}, u32[]{:S(2)}) collective-permute-start(bf16[1056,128]{1,0:T(8,128)(2,1)S(1)} %pack_payload.1.payload_ref.refs_0_), channel_id=1, source_target_pairs={{2,5},{3,4},{6,9},{7,8},{10,13},{11,12},{14,17},{15,16},{18,21},{1... | collective-permute-start | bytes 811016 | tf_op jit(solution)/shard_map/ppermute | solution.py:321
  4.5 3.7 %collective-permute-start.2 = (bf16[1056,128]{1,0:T(8,128)(2,1)S(1)}, bf16[1056,128]{1,0:T(8,128)(2,1)S(1)}, u32[]{:S(2)}, u32[]{:S(2)}) collective-permute-start(bf16[1056,128]{1,0:T(8,128)(2,1)S(1)} %pack_payload.1.payload_ref.refs_0_), channel_id=1, source_target_pairs={{2,0},{4,2},{6,4},{8,6},{10,8},{12,10},{14,12},{16,14},{18,16},{20... | collective-permute-start | bytes 811016 | tf_op jit(solution)/shard_map/ppermute | solution.py:323
  8.2 0.0 collective-permute-start.1
  8.2 0.5 %collective-permute-start = (bf16[1056,128]{1,0:T(8,128)(2,1)S(1)}, bf16[1056,128]{1,0:T(8,128)(2,1)S(1)}, u32[]{:S(2)}, u32[]{:S(2)}) collective-permute-start(bf16[1056,128]{1,0:T(8,128)(2,1)S(1)} %pack_payload.1.payload_ref.refs_0_), channel_id=1, source_target_pairs={{0,1},{1,0},{2,3},{3,2},{4,5},{5,4},{6,7},{7,6},{8,9},{9,8},{10,11... | collective-permute-start | bytes 811016 | tf_op jit(solution)/shard_map/ppermute | solution.py:324
  8.7 8.4 %left_sums.1.lefts_ref = bf16[6,128,2048]{2,1,0:T(8,128)(2,1)S(1)} custom-call(s32[32,27]{1,0:T(8,128)} %columns_hbm.1, s32[32]{0:T(128)} %counts_hbm.1, s32[32]{0:T(128)} %aggregate_hbm.3, bf16[1056,128]{1,0:T(8,128)(2,1)S(1)} %pack_payload.1.payload_ref.refs_0_, bf16[2,16,64,1728]{3,2,1,0:T(8,128)(2,1)} %bitcast.1), custom_call_target="tpu_custom_call" | custom-call | flops 9059696640 | bytes 12582912 | tf_op jit(solution)/shard_map/left_sums/pallas_call | solution.py:219
  17.1 0.5 %collective-permute-done.refs_1_ = bf16[1056,128]{1,0:T(8,128)(2,1)S(1)} collective-permute-done((bf16[1056,128]{1,0:T(8,128)(2,1)S(1)}, bf16[1056,128]{1,0:T(8,128)(2,1)S(1)}, u32[]{:S(2)}, u32[]{:S(2)}) %collective-permute-start) | collective-permute-done | bytes 270368 | tf_op jit(solution)/shard_map/ppermute | solution.py:324
  17.7 0.0 collective-permute-start.3
  17.7 0.0 collective-permute-done.4.refs_5_
  17.7 0.0 collective-permute-done.2.refs_3_
  17.7 0.0 collective-permute-done.1.refs_2_
  17.7 1.5 %collective-permute-done.3.refs_4_ = bf16[1056,128]{1,0:T(8,128)(2,1)S(1)} collective-permute-done((bf16[1056,128]{1,0:T(8,128)(2,1)S(1)}, bf16[1056,128]{1,0:T(8,128)(2,1)S(1)}, u32[]{:S(2)}, u32[]{:S(2)}) %collective-permute-start.3) | collective-permute-done | bytes 270368 | tf_op jit(solution)/shard_map/ppermute | solution.py:327
  19.2 1.8 %right_products.1 = f32[2,64,768]{2,1,0:T(8,128)} custom-call(bf16[6,128,2048]{2,1,0:T(8,128)(2,1)S(1)} %left_sums.1.lefts_ref, bf16[1056,128]{1,0:T(8,128)(2,1)S(1)} %pack_payload.1.payload_ref.refs_0_, bf16[1056,128]{1,0:T(8,128)(2,1)S(1)} %collective-permute-done.refs_1_, bf16[1056,128]{1,0:T(8,128)(2,1)S(1)} %collective-permute-done.1.refs_2_, ...), custom_call_target="tpu_custom_call" | custom-call | flops 402653184 | bytes 393216 | tf_op jit(solution)/shard_map/right_products/pallas_call | solution.py:289
Async XLA Ops:
  1.5 16.2 %collective-permute-start.4 = (bf16[1056,128]{1,0:T(8,128)(2,1)S(1)}, bf16[1056,128]{1,0:T(8,128)(2,1)S(1)}, u32[]{:S(2)}, u32[]{:S(2)}) collective-permute-start(bf16[1056,128]{1,0:T(8,128)(2,1)S(1)} %pack_payload.1.payload_ref.refs_0_), channel_id=1, source_target_pairs={{2,5},{3,4},{6,9},{7,8},{10,13},{11,12},{14,17},{15,16},{18,21},{1... | collective-permute-start | bytes 811016 | tf_op jit(solution)/shard_map/ppermute | solution.py:321
  4.5 13.1 %collective-permute-start.2 = (bf16[1056,128]{1,0:T(8,128)(2,1)S(1)}, bf16[1056,128]{1,0:T(8,128)(2,1)S(1)}, u32[]{:S(2)}, u32[]{:S(2)}) collective-permute-start(bf16[1056,128]{1,0:T(8,128)(2,1)S(1)} %pack_payload.1.payload_ref.refs_0_), channel_id=1, source_target_pairs={{2,0},{4,2},{6,4},{8,6},{10,8},{12,10},{14,12},{16,14},{18,16},{20... | collective-permute-start | bytes 811016 | tf_op jit(solution)/shard_map/ppermute | solution.py:323
  8.2 9.5 %collective-permute-start.1 = (bf16[1056,128]{1,0:T(8,128)(2,1)S(1)}, bf16[1056,128]{1,0:T(8,128)(2,1)S(1)}, u32[]{:S(2)}, u32[]{:S(2)}) collective-permute-start(bf16[1056,128]{1,0:T(8,128)(2,1)S(1)} %pack_payload.1.payload_ref.refs_0_), channel_id=1, source_target_pairs={{0,2},{2,4},{4,6},{6,8},{8,10},{10,12},{12,14},{14,16},{16,18},{18... | collective-permute-start | bytes 811016 | tf_op jit(solution)/shard_map/ppermute | solution.py:322
  8.2 9.4 %collective-permute-start = (bf16[1056,128]{1,0:T(8,128)(2,1)S(1)}, bf16[1056,128]{1,0:T(8,128)(2,1)S(1)}, u32[]{:S(2)}, u32[]{:S(2)}) collective-permute-start(bf16[1056,128]{1,0:T(8,128)(2,1)S(1)} %pack_payload.1.payload_ref.refs_0_), channel_id=1, source_target_pairs={{0,1},{1,0},{2,3},{3,2},{4,5},{5,4},{6,7},{7,6},{8,9},{9,8},{10,11... | collective-permute-start | bytes 811016 | tf_op jit(solution)/shard_map/ppermute | solution.py:324
  17.7 1.5 %collective-permute-start.3 = (bf16[1056,128]{1,0:T(8,128)(2,1)S(1)}, bf16[1056,128]{1,0:T(8,128)(2,1)S(1)}, u32[]{:S(2)}, u32[]{:S(2)}) collective-permute-start(bf16[1056,128]{1,0:T(8,128)(2,1)S(1)} %collective-permute-done.refs_1_), channel_id=1, source_target_pairs={{0,2},{2,0},{4,6},{6,4},{8,10},{10,8},{12,14},{14,12},{16,18},{18,... | collective-permute-start | bytes 811016 | tf_op jit(solution)/shard_map/ppermute | solution.py:327

commit v3 on v2

--- a/solution.py
+++ b/solution.py
@@ -14,12 +14,10 @@
 
 LANES = 2 * BLK
 PAIRS = ROWS_DEV // 2
-HALF = PAIRS // 2
-TAG = 16
-HALF_ROWS = HALF * BLK + TAG
-PAYLOAD = 2 * HALF_ROWS
+TAGS = PAIRS * BLK
+PAYLOAD = TAGS + PAIRS
 STEP = 4
-DEPTH = 2
+BATCH = 4
 CHUNK = 6
 MIB = 1 << 20
 
@@ -30,19 +28,14 @@
     rows.start()
     tags.start()
     tags.wait()
-    row = lax.broadcasted_iota(jnp.int32, (TAG, LANES), 0)
-    low = lax.broadcasted_iota(jnp.int32, (TAG, LANES), 1) < BLK
-    for half in range(2):
-        owners = jnp.zeros((TAG, LANES), jnp.int32)
-        for p in range(HALF):
-            g = half * HALF + p
-            owners = jnp.where(
-                row == p, jnp.where(low, aggregate_ref[g], aggregate_ref[g + PAIRS]), owners
-            )
-        last = (half + 1) * HALF_ROWS
-        out_ref[last - TAG : last, :] = owners.astype(jnp.float32).astype(jnp.bfloat16)
+    row = lax.broadcasted_iota(jnp.int32, (PAIRS, LANES), 0)
+    low = lax.broadcasted_iota(jnp.int32, (PAIRS, LANES), 1) < BLK
+    owners = jnp.zeros((PAIRS, LANES), jnp.int32)
+    for p in range(PAIRS):
+        owner = jnp.where(low, aggregate_ref[p], aggregate_ref[p + PAIRS])
+        owners = jnp.where(row == p, owner, owners)
+    out_ref[TAGS:, :] = owners.astype(jnp.float32).astype(jnp.bfloat16)
     rows.wait()
-    low = lax.broadcasted_iota(jnp.int32, (PAIRS, LANES), 1) < BLK
     for t in range(BLK // 2):
         x = restrict_ref[:, t * LANES : (t + 1) * LANES].astype(jnp.float32)
         first, second = x[:PAIRS], x[PAIRS:]
@@ -50,10 +43,7 @@
         odd = jnp.where(low, pltpu.roll(first, BLK, 1), second)
         wide_ref[pl.ds(2 * t, PAIRS, stride=BLK), :] = even
         wide_ref[pl.ds(2 * t + 1, PAIRS, stride=BLK), :] = odd
-    for half in range(2):
-        out_ref[half * HALF_ROWS : half * HALF_ROWS + HALF * BLK, :] = wide_ref[
-            half * HALF * BLK : (half + 1) * HALF * BLK, :
-        ].astype(jnp.bfloat16)
+    out_ref[:TAGS, :] = wide_ref[...].astype(jnp.bfloat16)
 
 
 def pack(aggregate, restrict):
@@ -116,23 +106,19 @@
     low_short = lax.broadcasted_iota(jnp.int32, (short, LANES), 1) < BLK
 
     def add_all(entries):
-        waiting = []
-        for place, tile in entries:
-            value = sums_ref[place]
-            for earlier, earlier_value in waiting:
-                value = jnp.where(place == earlier, earlier_value, value)
-            value = value + tile
-            if len(waiting) == DEPTH:
-                sums_ref[waiting[0][0]] = waiting[0][1]
-                waiting = waiting[1:]
-            waiting = waiting + [(place, value)]
-        for place, value in waiting:
-            sums_ref[place] = value
+        entries = list(entries)
+        for first in range(0, len(entries), BATCH):
+            batch = entries[first : first + BATCH]
+            values = [sums_ref[place] for place, _ in batch]
+            for n, (place, tile) in enumerate(batch):
+                for earlier in range(n):
+                    values[n] = jnp.where(place == batch[earlier][0], values[earlier], values[n])
+                values[n] = values[n] + tile
+            for (place, _), value in zip(batch, values):
+                sums_ref[place] = value
 
     def tiles_of(base, pair):
-        half = pair // HALF
-        start = pl.multiple_of(half * HALF_ROWS + (pair - half * HALF) * BLK, 16)
-        both = payload_ref[pl.ds(start, BLK), :]
+        both = payload_ref[pl.ds(pl.multiple_of(pair * BLK, BLK), BLK), :]
         zero = jnp.zeros_like(both)
         lhs = jnp.concatenate([jnp.where(low, both, zero), jnp.where(low, zero, both)], axis=0)
         rows = (pair, pair + PAIRS)
@@ -232,7 +218,7 @@
         ],
         compiler_params=pltpu.CompilerParams(vmem_limit_bytes=20 * MIB),
         cost_estimate=pl.CostEstimate(
-            flops=40 * ROWS_DEV * SLOTS * BLK**3, bytes_accessed=12 * MIB, transcendentals=0
+            flops=4 * ROWS_DEV * SLOTS * BLK**3, bytes_accessed=4 * MIB // 2, transcendentals=0
         ),
         name="left_sums",
     )(
@@ -242,56 +228,61 @@
     )
 
 
-def half_product(lefts, half, piece):
-    tags = piece[HALF * BLK : HALF_ROWS, :].astype(jnp.float32)
+def block_product(lefts, piece):
+    tags = piece[TAGS:, :].astype(jnp.float32)
     masks = [(tags == j).astype(jnp.float32).astype(jnp.bfloat16) for j in range(AGG_DEV)]
     rhs = jnp.concatenate(
         [
             jnp.concatenate(
-                [piece[p * BLK : (p + 1) * BLK, :] * masks[j][p : p + 1, :] for p in range(HALF)],
+                [piece[p * BLK : (p + 1) * BLK, :] * masks[j][p : p + 1, :] for p in range(PAIRS)],
                 axis=1,
             )
             for j in range(AGG_DEV)
         ],
         axis=0,
     )
-    cut = lefts[:, half * HALF * LANES : (half + 1) * HALF * LANES]
     return lax.dot_general(
-        cut, rhs, (((1,), (1,)), ((), ())), preferred_element_type=jnp.float32
+        lefts, rhs, (((1,), (1,)), ((), ())), preferred_element_type=jnp.float32
     )
 
 
 def right_kernel(sources, order, first, carried, lefts_ref, *refs):
-    out_ref = refs[-1]
-    if carried:
-        out_ref[...] = refs[-2][...]
-    places = order()
-    for position, halves in enumerate(sources):
-        lefts = lefts_ref[first + position]
-        total = 0.0
-        for half, (index, start) in enumerate(halves):
-            piece = refs[index][start : start + HALF_ROWS, :]
-            total = total + half_product(lefts, half, piece)
-        place, _ = places[first + position]
-        if not isinstance(place, int):
-            place = pl.multiple_of(place * LANES, LANES)
-        else:
-            place = place * LANES
+    refs = list(refs)
+    before = refs.pop(-4) if carried else None
+    out_hbm, columns_ref, sems = refs[-3:]
+    copies = []
+    for position, (index, start) in enumerate(sources):
+        total = block_product(
+            lefts_ref[first + position], refs[index][start : start + PAYLOAD, :]
+        )
+        place, _ = order()[first + position]
+        place = place * LANES if isinstance(place, int) else pl.multiple_of(place * LANES, LANES)
         for a in range(AGG_DEV):
-            out_ref[a, :, pl.ds(place, LANES)] = total[a * BLK : (a + 1) * BLK]
-
-
-def right_products(lefts, pieces, sources, order, first, width, so_far, last):
+            columns_ref[position, a] = total[a * BLK : (a + 1) * BLK]
+        copy = pltpu.make_async_copy(
+            columns_ref.at[position], out_hbm.at[:, :, pl.ds(place, LANES)], sems.at[position]
+        )
+        copy.start()
+        copies.append(copy)
+    for copy in copies:
+        copy.wait()
+
+
+def right_products(lefts, pieces, sources, order, first, width, so_far):
     carried = so_far is not None
     many = len(sources)
     vmem = pl.BlockSpec(memory_space=pltpu.VMEM)
-    shape = jax.ShapeDtypeStruct((AGG_DEV, BLK, width), jnp.float32)
+    hbm = pl.BlockSpec(memory_space=pltpu.HBM)
     return pl.pallas_call(
         functools.partial(right_kernel, sources, order, first, carried),
-        grid=(1,),
-        out_shape=shape,
-        in_specs=[vmem] * (1 + len(pieces) + carried),
-        out_specs=pl.BlockSpec(shape.shape, lambda s: (0, 0, 0)) if last else vmem,
+        out_shape=jax.ShapeDtypeStruct((AGG_DEV, BLK, width), jnp.float32),
+        in_specs=[vmem] * (1 + len(pieces)) + [hbm] * carried,
+        out_specs=hbm,
+        scratch_shapes=[
+            pltpu.VMEM((many, AGG_DEV, BLK, LANES), jnp.float32),
+            pltpu.SemaphoreType.DMA((many,)),
+        ],
+        input_output_aliases={1 + len(pieces): 0} if carried else {},
         compiler_params=pltpu.CompilerParams(vmem_limit_bytes=8 * MIB),
         cost_estimate=pl.CostEstimate(
             flops=2 * many * (AGG_DEV * BLK) ** 2 * PAIRS * LANES,
@@ -319,22 +310,20 @@
         return [(2 * slab + col, live) for (slab, col), live in zip(spots, [None, None, inside[0], inside[2], None, far])]
 
     far = lax.ppermute(payload, ("rows", "cols"), crossed)
+    beside = lax.ppermute(payload, "cols", across)
     below = lax.ppermute(payload, "rows", ring)
     above = lax.ppermute(payload, "rows", [(b, a) for a, b in ring])
-    beside = lax.ppermute(payload, "cols", across)
     lefts = left_sums(columns, counts, aggregate, payload, matrix_blocks, 6, order)
     lefts, beside = lax.optimization_barrier((lefts, beside))
     inner = lax.ppermute(beside, "rows", evens)
-    whole = lambda index: ((index, 0), (index, HALF_ROWS))
     return right_products(
         lefts,
         [payload, beside, below, above, inner, far],
-        [whole(index) for index in range(6)],
+        [(index, 0) for index in range(6)],
         order,
         0,
         6 * LANES,
         None,
-        True,
     )
 
 
@@ -346,12 +335,8 @@
     total = 3 * col_count
     order = lambda: [(block, None) for block in range(total)]
     lefts = left_sums(columns, counts, aggregate, payload, matrix_blocks, total, lambda: None)
-    sources = [
-        tuple((s, (c * 2 + half) * HALF_ROWS) for half in range(2))
-        for s in range(3)
-        for c in range(col_count)
-    ]
-    return right_products(lefts, pieces, sources, order, 0, total * LANES, None, True)
+    sources = [(slab, c * PAYLOAD) for slab in range(3) for c in range(col_count)]
+    return right_products(lefts, pieces, sources, order, 0, total * LANES, None)
 
 
 def per_device(matrix_blocks, restrict, columns, counts, aggregate):

time: 21.1 us -> 19.5 us (0.924)
  the two profiles are of different devices: /device:TPU:0 before, /device:TPU:1 now
where the time goes in v3:
time: 19.5 us; the launch traced here: 19.4 us
  Pallas kernels  10.1 us (52%)
  starting transfers between devices  7.1 us (36%)
  waiting for transfers between devices  2.15 us (11%)
    pallas_call x1, Pallas kernels, left_sums(): pl.pallas_call(functools.partial(left_kernel, order), out_shape=jax.Shape...  6.87 us
    ppermute x1, waiting for transfers between devices, paired_plan(): below = lax.ppermute(payload, 'rows', ring)  2.14 us
    ppermute x1, starting transfers between devices, paired_plan(): beside = lax.ppermute(payload, 'cols', across)  2.13 us
    ppermute x1, starting transfers between devices, paired_plan(): far = lax.ppermute(payload, ('rows', 'cols'), crossed)  1.99 us
    ppermute x1, starting transfers between devices, paired_plan(): below = lax.ppermute(payload, 'rows', ring)  1.74 us
    pallas_call x1, Pallas kernels, right_products(): pl.pallas_call(functools.partial(right_kernel, sources, order, first, car...  1.72 us
    pallas_call x1, Pallas kernels, pack(): pl.pallas_call(pack_kernel, out_shape=jax.ShapeDtypeStruct((PAYLOAD, LANE...  1.49 us
    ppermute x1, starting transfers between devices, paired_plan(): inner = lax.ppermute(beside, 'rows', evens)  1.23 us
  transfers between devices with their start and end apart: 5, of which 1 were waited for; matrix products, arithmetic and copies ran while one was open for 0% of the time, Pallas kernels for 35%

profile of v3, /device:TPU:1, one launch (start us, length us, event | category | flops | bytes accessed | tf_op | source)
XLA Modules:
  0.0 19.4 jit_solution(1630011001307196165)
XLA Ops:
  0.0 1.5 %pack_payload.1.payload_ref.refs_0_ = bf16[1040,128]{1,0:T(8,128)(2,1)S(1)} custom-call(s32[32]{0:T(128)} %aggregate_hbm.3, bf16[32,4096]{1,0:T(8,128)(2,1)} %restrict_hbm.1), custom_call_target="tpu_custom_call" | custom-call | tf_op jit(solution)/shard_map/pack_payload/pallas_call | solution.py:51
  1.5 2.1 %collective-permute-start = (bf16[1040,128]{1,0:T(8,128)(2,1)S(1)}, bf16[1040,128]{1,0:T(8,128)(2,1)S(1)}, u32[]{:S(2)}, u32[]{:S(2)}) collective-permute-start(bf16[1040,128]{1,0:T(8,128)(2,1)S(1)} %pack_payload.1.payload_ref.refs_0_), channel_id=1, source_target_pairs={{0,1},{1,0},{2,3},{3,2},{4,5},{5,4},{6,7},{7,6},{8,9},{9,8},{10,11... | collective-permute-start | bytes 798728 | tf_op jit(solution)/shard_map/ppermute | solution.py:313
  3.6 2.0 %collective-permute-start.4 = (bf16[1040,128]{1,0:T(8,128)(2,1)S(1)}, bf16[1040,128]{1,0:T(8,128)(2,1)S(1)}, u32[]{:S(2)}, u32[]{:S(2)}) collective-permute-start(bf16[1040,128]{1,0:T(8,128)(2,1)S(1)} %pack_payload.1.payload_ref.refs_0_), channel_id=1, source_target_pairs={{2,5},{3,4},{6,9},{7,8},{10,13},{11,12},{14,17},{15,16},{18,21},{1... | collective-permute-start | bytes 798728 | tf_op jit(solution)/shard_map/ppermute | solution.py:312
  5.6 0.0 collective-permute-start.2
  5.6 1.7 %collective-permute-start.1 = (bf16[1040,128]{1,0:T(8,128)(2,1)S(1)}, bf16[1040,128]{1,0:T(8,128)(2,1)S(1)}, u32[]{:S(2)}, u32[]{:S(2)}) collective-permute-start(bf16[1040,128]{1,0:T(8,128)(2,1)S(1)} %pack_payload.1.payload_ref.refs_0_), channel_id=1, source_target_pairs={{0,2},{2,4},{4,6},{6,8},{8,10},{10,12},{12,14},{14,16},{16,18},{18... | collective-permute-start | bytes 798728 | tf_op jit(solution)/shard_map/ppermute | solution.py:314
  7.4 6.9 %left_sums.1.lefts_ref = bf16[6,128,2048]{2,1,0:T(8,128)(2,1)S(1)} custom-call(s32[32,27]{1,0:T(8,128)} %columns_hbm.1, s32[32]{0:T(128)} %counts_hbm.1, s32[32]{0:T(128)} %aggregate_hbm.3, bf16[1040,128]{1,0:T(8,128)(2,1)S(1)} %pack_payload.1.payload_ref.refs_0_, bf16[2,16,64,1728]{3,2,1,0:T(8,128)(2,1)} %bitcast.1), custom_call_target="tpu_custom_call" | custom-call | flops 905969664 | bytes 2097152 | tf_op jit(solution)/shard_map/left_sums/pallas_call | solution.py:205
  14.3 0.0 collective-permute-done.refs_1_
  14.3 1.2 %collective-permute-start.3 = (bf16[1040,128]{1,0:T(8,128)(2,1)S(1)}, bf16[1040,128]{1,0:T(8,128)(2,1)S(1)}, u32[]{:S(2)}, u32[]{:S(2)}) collective-permute-start(bf16[1040,128]{1,0:T(8,128)(2,1)S(1)} %collective-permute-done.refs_1_), channel_id=1, source_target_pairs={{0,2},{2,0},{4,6},{6,4},{8,10},{10,8},{12,14},{14,12},{16,18},{18,... | collective-permute-start | bytes 798728 | tf_op jit(solution)/shard_map/ppermute | solution.py:318
  15.5 0.0 collective-permute-done.4.refs_5_
  15.5 0.0 collective-permute-done.2.refs_3_
  15.5 2.1 %collective-permute-done.1.refs_2_ = bf16[1040,128]{1,0:T(8,128)(2,1)S(1)} collective-permute-done((bf16[1040,128]{1,0:T(8,128)(2,1)S(1)}, bf16[1040,128]{1,0:T(8,128)(2,1)S(1)}, u32[]{:S(2)}, u32[]{:S(2)}) %collective-permute-start.1) | collective-permute-done | bytes 266272 | tf_op jit(solution)/shard_map/ppermute | solution.py:314
  17.6 0.0 collective-permute-done.3.refs_4_
  17.6 1.7 %right_products.1 = f32[2,64,768]{2,1,0:T(8,128)} custom-call(bf16[6,128,2048]{2,1,0:T(8,128)(2,1)S(1)} %left_sums.1.lefts_ref, bf16[1040,128]{1,0:T(8,128)(2,1)S(1)} %pack_payload.1.payload_ref.refs_0_, bf16[1040,128]{1,0:T(8,128)(2,1)S(1)} %collective-permute-done.refs_1_, bf16[1040,128]{1,0:T(8,128)(2,1)S(1)} %collective-permute-done.1.refs_2_, ...), custom_call_target="tpu_custom_call" | custom-call | flops 402653184 | bytes 393216 | tf_op jit(solution)/shard_map/right_products/pallas_call | solution.py:276
Async XLA Ops:
  1.5 12.8 %collective-permute-start = (bf16[1040,128]{1,0:T(8,128)(2,1)S(1)}, bf16[1040,128]{1,0:T(8,128)(2,1)S(1)}, u32[]{:S(2)}, u32[]{:S(2)}) collective-permute-start(bf16[1040,128]{1,0:T(8,128)(2,1)S(1)} %pack_payload.1.payload_ref.refs_0_), channel_id=1, source_target_pairs={{0,1},{1,0},{2,3},{3,2},{4,5},{5,4},{6,7},{7,6},{8,9},{9,8},{10,11... | collective-permute-start | bytes 798728 | tf_op jit(solution)/shard_map/ppermute | solution.py:313
  3.6 11.9 %collective-permute-start.4 = (bf16[1040,128]{1,0:T(8,128)(2,1)S(1)}, bf16[1040,128]{1,0:T(8,128)(2,1)S(1)}, u32[]{:S(2)}, u32[]{:S(2)}) collective-permute-start(bf16[1040,128]{1,0:T(8,128)(2,1)S(1)} %pack_payload.1.payload_ref.refs_0_), channel_id=1, source_target_pairs={{2,5},{3,4},{6,9},{7,8},{10,13},{11,12},{14,17},{15,16},{18,21},{1... | collective-permute-start | bytes 798728 | tf_op jit(solution)/shard_map/ppermute | solution.py:312
  5.6 9.9 %collective-permute-start.2 = (bf16[1040,128]{1,0:T(8,128)(2,1)S(1)}, bf16[1040,128]{1,0:T(8,128)(2,1)S(1)}, u32[]{:S(2)}, u32[]{:S(2)}) collective-permute-start(bf16[1040,128]{1,0:T(8,128)(2,1)S(1)} %pack_payload.1.payload_ref.refs_0_), channel_id=1, source_target_pairs={{2,0},{4,2},{6,4},{8,6},{10,8},{12,10},{14,12},{16,14},{18,16},{20... | collective-permute-start | bytes 798728 | tf_op jit(solution)/shard_map/ppermute | solution.py:315
  5.6 12.0 %collective-permute-start.1 = (bf16[1040,128]{1,0:T(8,128)(2,1)S(1)}, bf16[1040,128]{1,0:T(8,128)(2,1)S(1)}, u32[]{:S(2)}, u32[]{:S(2)}) collective-permute-start(bf16[1040,128]{1,0:T(8,128)(2,1)S(1)} %pack_payload.1.payload_ref.refs_0_), channel_id=1, source_target_pairs={{0,2},{2,4},{4,6},{6,8},{8,10},{10,12},{12,14},{14,16},{16,18},{18... | collective-permute-start | bytes 798728 | tf_op jit(solution)/shard_map/ppermute | solution.py:314
  14.3 3.4 %collective-permute-start.3 = (bf16[1040,128]{1,0:T(8,128)(2,1)S(1)}, bf16[1040,128]{1,0:T(8,128)(2,1)S(1)}, u32[]{:S(2)}, u32[]{:S(2)}) collective-permute-start(bf16[1040,128]{1,0:T(8,128)(2,1)S(1)} %collective-permute-done.refs_1_), channel_id=1, source_target_pairs={{0,2},{2,0},{4,6},{6,4},{8,10},{10,8},{12,14},{14,12},{16,18},{18,... | collective-permute-start | bytes 798728 | tf_op jit(solution)/shard_map/ppermute | solution.py:318

commit v4 on v3

--- a/solution.py
+++ b/solution.py
@@ -246,51 +246,79 @@
     )
 
 
-def right_kernel(sources, order, first, carried, lefts_ref, *refs):
-    refs = list(refs)
-    before = refs.pop(-4) if carried else None
+def near_kernel(first, lefts_ref, *refs):
+    out_ref = refs[-1]
+    for position, piece in enumerate(refs[:-1]):
+        total = block_product(lefts_ref[first + position], piece[...])
+        for a in range(AGG_DEV):
+            out_ref[position, a] = total[a * BLK : (a + 1) * BLK]
+
+
+def near_products(lefts, pieces, first):
+    many = len(pieces)
+    vmem = pl.BlockSpec(memory_space=pltpu.VMEM)
+    return pl.pallas_call(
+        functools.partial(near_kernel, first),
+        out_shape=jax.ShapeDtypeStruct((many, AGG_DEV, BLK, LANES), jnp.float32),
+        in_specs=[vmem] * (1 + many),
+        out_specs=vmem,
+        compiler_params=pltpu.CompilerParams(vmem_limit_bytes=8 * MIB),
+        cost_estimate=right_cost(many),
+        name="near_products",
+    )(lefts, *pieces)
+
+
+def right_cost(many):
+    return pl.CostEstimate(
+        flops=2 * many * (AGG_DEV * BLK) ** 2 * PAIRS * LANES,
+        bytes_accessed=many * MIB // 16,
+        transcendentals=0,
+    )
+
+
+def right_kernel(sources, order, first, lefts_ref, *refs):
     out_hbm, columns_ref, sems = refs[-3:]
     copies = []
+
+    def send(position, tile):
+        place, _ = order()[position]
+        place = place * LANES if isinstance(place, int) else pl.multiple_of(place * LANES, LANES)
+        copy = pltpu.make_async_copy(
+            tile, out_hbm.at[:, :, pl.ds(place, LANES)], sems.at[position]
+        )
+        copy.start()
+        copies.append(copy)
+
+    for position in range(first):
+        send(position, refs[-4].at[position])
     for position, (index, start) in enumerate(sources):
         total = block_product(
             lefts_ref[first + position], refs[index][start : start + PAYLOAD, :]
         )
-        place, _ = order()[first + position]
-        place = place * LANES if isinstance(place, int) else pl.multiple_of(place * LANES, LANES)
         for a in range(AGG_DEV):
             columns_ref[position, a] = total[a * BLK : (a + 1) * BLK]
-        copy = pltpu.make_async_copy(
-            columns_ref.at[position], out_hbm.at[:, :, pl.ds(place, LANES)], sems.at[position]
-        )
-        copy.start()
-        copies.append(copy)
+        send(first + position, columns_ref.at[position])
     for copy in copies:
         copy.wait()
 
 
-def right_products(lefts, pieces, sources, order, first, width, so_far):
-    carried = so_far is not None
+def right_products(lefts, pieces, sources, order, width, near):
+    first = 0 if near is None else near.shape[0]
     many = len(sources)
     vmem = pl.BlockSpec(memory_space=pltpu.VMEM)
-    hbm = pl.BlockSpec(memory_space=pltpu.HBM)
     return pl.pallas_call(
-        functools.partial(right_kernel, sources, order, first, carried),
+        functools.partial(right_kernel, sources, order, first),
         out_shape=jax.ShapeDtypeStruct((AGG_DEV, BLK, width), jnp.float32),
-        in_specs=[vmem] * (1 + len(pieces)) + [hbm] * carried,
-        out_specs=hbm,
+        in_specs=[vmem] * (1 + len(pieces) + (first > 0)),
+        out_specs=pl.BlockSpec(memory_space=pltpu.HBM),
         scratch_shapes=[
             pltpu.VMEM((many, AGG_DEV, BLK, LANES), jnp.float32),
-            pltpu.SemaphoreType.DMA((many,)),
+            pltpu.SemaphoreType.DMA((first + many,)),
         ],
-        input_output_aliases={1 + len(pieces): 0} if carried else {},
         compiler_params=pltpu.CompilerParams(vmem_limit_bytes=8 * MIB),
-        cost_estimate=pl.CostEstimate(
-            flops=2 * many * (AGG_DEV * BLK) ** 2 * PAIRS * LANES,
-            bytes_accessed=many * MIB // 16,
-            transcendentals=0,
-        ),
+        cost_estimate=right_cost(many),
         name="right_products",
-    )(lefts, *pieces, *([so_far] if carried else []))
+    )(lefts, *pieces, *([near] if first else []))
 
 
 def paired_plan(columns, counts, aggregate, matrix_blocks, payload, row_count):
@@ -304,10 +332,16 @@
     def order():
         c, row = lax.axis_index("cols"), lax.axis_index("rows")
         up = 1 - lax.rem(row, 2)
-        inside = [row > 0, None, row < row_count - 1]
-        spots = [(1, c), (1, 1 - c), (0, c), (2, c), (2 * up, 1 - c), (2 - 2 * up, 1 - c)]
-        far = (up == 0) & (row < row_count - 1) | (up == 1) & (row > 0)
-        return [(2 * slab + col, live) for (slab, col), live in zip(spots, [None, None, inside[0], inside[2], None, far])]
+        low, high = row > 0, row < row_count - 1
+        far = (up == 0) & high | (up == 1) & low
+        return [
+            (2 + c, None),
+            (3 - c, None),
+            (4 - 4 * up + 1 - c, far),
+            (4 * up + 1 - c, None),
+            (c, low),
+            (4 + c, high),
+        ]
 
     far = lax.ppermute(payload, ("rows", "cols"), crossed)
     beside = lax.ppermute(payload, "cols", across)
@@ -316,15 +350,9 @@
     lefts = left_sums(columns, counts, aggregate, payload, matrix_blocks, 6, order)
     lefts, beside = lax.optimization_barrier((lefts, beside))
     inner = lax.ppermute(beside, "rows", evens)
-    return right_products(
-        lefts,
-        [payload, beside, below, above, inner, far],
-        [(index, 0) for index in range(6)],
-        order,
-        0,
-        6 * LANES,
-        None,
-    )
+    near = near_products(lefts, [payload, beside, far], 0)
+    sources = [(index, 0) for index in range(3)]
+    return right_products(lefts, [inner, below, above], sources, order, 6 * LANES, near)
 
 
 def general_plan(columns, counts, aggregate, matrix_blocks, payload, row_count, col_count):
@@ -336,7 +364,7 @@
     order = lambda: [(block, None) for block in range(total)]
     lefts = left_sums(columns, counts, aggregate, payload, matrix_blocks, total, lambda: None)
     sources = [(slab, c * PAYLOAD) for slab in range(3) for c in range(col_count)]
-    return right_products(lefts, pieces, sources, order, 0, total * LANES, None)
+    return right_products(lefts, pieces, sources, order, total * LANES, None)
 
 
 def per_device(matrix_blocks, restrict, columns, counts, aggregate):

time: 19.5 us -> 19.1 us (0.979)
  waiting for transfers between devices: 2.15 us -> 1 us
  starting transfers between devices: 7.1 us -> 7.63 us
  Pallas kernels: 10.1 us -> 10.3 us
    ppermute x1, starting transfers between devices: 1.23 us -> 2.99 us  [paired_plan(): inner = lax.ppermute(beside, 'rows', evens)]
    ppermute x1, starting transfers between devices: 1.74 us -> 0.06 us  [paired_plan(): below = lax.ppermute(payload, 'rows', ring)]
    ppermute x1, waiting for transfers between devices: 2.14 us -> 0.99 us  [paired_plan(): below = lax.ppermute(payload, 'rows', ring)]
    ppermute x1, starting transfers between devices: 0.01 us -> 0.45 us  [paired_plan(): above = lax.ppermute(payload, 'rows', [(b, a) for a, b in ring])]
    pallas_call x1 -> x2, Pallas kernels: 1.72 us -> 1.87 us  [the longest x1 1.29 us: right_products(): pl.pallas_call(functools.partial(right_kernel, sources, order, first), ou...]
  transfers between devices with their start and end apart: 5 -> 5, of which waited for: 1 -> 1; matrix products, arithmetic and copies ran while one was open for 0% -> 0% of each run, Pallas kernels for 35% -> 40%
where the time goes in v4:
time: 19.1 us; the launch traced here: 18.9 us
  Pallas kernels  10.3 us (54%)
  starting transfers between devices  7.63 us (40%)
  waiting for transfers between devices  1 us (5%)
    pallas_call x1, Pallas kernels, left_sums(): pl.pallas_call(functools.partial(left_kernel, order), out_shape=jax.Shape...  6.91 us
    ppermute x1, starting transfers between devices, paired_plan(): inner = lax.ppermute(beside, 'rows', evens)  2.99 us
    ppermute x1, starting transfers between devices, paired_plan(): beside = lax.ppermute(payload, 'cols', across)  2.13 us
    ppermute x1, starting transfers between devices, paired_plan(): far = lax.ppermute(payload, ('rows', 'cols'), crossed)  1.99 us
    pallas_call x1, Pallas kernels, pack(): pl.pallas_call(pack_kernel, out_shape=jax.ShapeDtypeStruct((PAYLOAD, LANE...  1.49 us
    pallas_call x1, Pallas kernels, right_products(): pl.pallas_call(functools.partial(right_kernel, sources, order, first), ou...  1.29 us
    ppermute x1, waiting for transfers between devices, paired_plan(): below = lax.ppermute(payload, 'rows', ring)  0.99 us
    pallas_call x1, Pallas kernels, near_products(): pl.pallas_call(functools.partial(near_kernel, first), out_shape=jax.Shape...  0.58 us
  transfers between devices with their start and end apart: 5, of which 1 were waited for; matrix products, arithmetic and copies ran while one was open for 0% of the time, Pallas kernels for 40%

profile of v4, /device:TPU:1, one launch (start us, length us, event | category | flops | bytes accessed | tf_op | source)
XLA Modules:
  0.0 18.9 jit_solution(12958596909611901036)
XLA Ops:
  0.0 1.5 %pack_payload.1.payload_ref.refs_0_ = bf16[1040,128]{1,0:T(8,128)(2,1)S(1)} custom-call(s32[32]{0:T(128)} %aggregate_hbm.3, bf16[32,4096]{1,0:T(8,128)(2,1)} %restrict_hbm.1), custom_call_target="tpu_custom_call" | custom-call | tf_op jit(solution)/shard_map/pack_payload/pallas_call | solution.py:51
  1.5 2.1 %collective-permute-start = (bf16[1040,128]{1,0:T(8,128)(2,1)S(1)}, bf16[1040,128]{1,0:T(8,128)(2,1)S(1)}, u32[]{:S(2)}, u32[]{:S(2)}) collective-permute-start(bf16[1040,128]{1,0:T(8,128)(2,1)S(1)} %pack_payload.1.payload_ref.refs_0_), channel_id=1, source_target_pairs={{0,1},{1,0},{2,3},{3,2},{4,5},{5,4},{6,7},{7,6},{8,9},{9,8},{10,11... | collective-permute-start | bytes 798728 | tf_op jit(solution)/shard_map/ppermute | solution.py:347
  3.6 2.0 %collective-permute-start.4 = (bf16[1040,128]{1,0:T(8,128)(2,1)S(1)}, bf16[1040,128]{1,0:T(8,128)(2,1)S(1)}, u32[]{:S(2)}, u32[]{:S(2)}) collective-permute-start(bf16[1040,128]{1,0:T(8,128)(2,1)S(1)} %pack_payload.1.payload_ref.refs_0_), channel_id=1, source_target_pairs={{2,5},{3,4},{6,9},{7,8},{10,13},{11,12},{14,17},{15,16},{18,21},{1... | collective-permute-start | bytes 798728 | tf_op jit(solution)/shard_map/ppermute | solution.py:346
  5.6 0.1 collective-permute-start.2
  5.7 0.5 %collective-permute-start.3 = (bf16[1040,128]{1,0:T(8,128)(2,1)S(1)}, bf16[1040,128]{1,0:T(8,128)(2,1)S(1)}, u32[]{:S(2)}, u32[]{:S(2)}) collective-permute-start(bf16[1040,128]{1,0:T(8,128)(2,1)S(1)} %pack_payload.1.payload_ref.refs_0_), channel_id=1, source_target_pairs={{2,0},{4,2},{6,4},{8,6},{10,8},{12,10},{14,12},{16,14},{18,16},{20... | collective-permute-start | bytes 798728 | tf_op jit(solution)/shard_map/ppermute | solution.py:349
  6.1 6.9 %left_sums.1.lefts_ref = bf16[6,128,2048]{2,1,0:T(8,128)(2,1)S(1)} custom-call(s32[32,27]{1,0:T(8,128)} %columns_hbm.1, s32[32]{0:T(128)} %counts_hbm.1, s32[32]{0:T(128)} %aggregate_hbm.3, bf16[1040,128]{1,0:T(8,128)(2,1)S(1)} %pack_payload.1.payload_ref.refs_0_, bf16[2,16,64,1728]{3,2,1,0:T(8,128)(2,1)} %bitcast.1), custom_call_target="tpu_custom_call" | custom-call | flops 905969664 | bytes 2097152 | tf_op jit(solution)/shard_map/left_sums/pallas_call | solution.py:205
  13.1 0.0 collective-permute-done.refs_1_
  13.1 3.0 %collective-permute-start.1 = (bf16[1040,128]{1,0:T(8,128)(2,1)S(1)}, bf16[1040,128]{1,0:T(8,128)(2,1)S(1)}, u32[]{:S(2)}, u32[]{:S(2)}) collective-permute-start(bf16[1040,128]{1,0:T(8,128)(2,1)S(1)} %collective-permute-done.refs_1_), channel_id=1, source_target_pairs={{0,2},{2,0},{4,6},{6,4},{8,10},{10,8},{12,14},{14,12},{16,18},{18,... | collective-permute-start | bytes 798728 | tf_op jit(solution)/shard_map/ppermute | solution.py:352
  16.1 0.0 collective-permute-done.4.refs_2_
  16.1 0.6 %near_products.1.refs_3_ = f32[3,2,64,128]{3,2,1,0:T(8,128)S(1)} custom-call(bf16[6,128,2048]{2,1,0:T(8,128)(2,1)S(1)} %left_sums.1.lefts_ref, bf16[1040,128]{1,0:T(8,128)(2,1)S(1)} %pack_payload.1.payload_ref.refs_0_, bf16[1040,128]{1,0:T(8,128)(2,1)S(1)} %collective-permute-done.refs_1_, bf16[1040,128]{1,0:T(8,128)(2,1)S(1)} %collective-permute-done.4.refs_2_), custom_call_target="tpu_custom_call" | custom-call | flops 201326592 | bytes 196608 | tf_op jit(solution)/shard_map/near_products/pallas_call | solution.py:260
  16.6 1.0 %collective-permute-done.2.refs_1_ = bf16[1040,128]{1,0:T(8,128)(2,1)S(1)} collective-permute-done((bf16[1040,128]{1,0:T(8,128)(2,1)S(1)}, bf16[1040,128]{1,0:T(8,128)(2,1)S(1)}, u32[]{:S(2)}, u32[]{:S(2)}) %collective-permute-start.2) | collective-permute-done | bytes 266272 | tf_op jit(solution)/shard_map/ppermute | solution.py:348
  17.6 0.0 collective-permute-done.3.refs_2_
  17.6 0.0 collective-permute-done.1.refs_0_
  17.6 1.3 %right_products.1 = f32[2,64,768]{2,1,0:T(8,128)} custom-call(bf16[6,128,2048]{2,1,0:T(8,128)(2,1)S(1)} %left_sums.1.lefts_ref, bf16[1040,128]{1,0:T(8,128)(2,1)S(1)} %collective-permute-done.1.refs_0_, bf16[1040,128]{1,0:T(8,128)(2,1)S(1)} %collective-permute-done.2.refs_1_, bf16[1040,128]{1,0:T(8,128)(2,1)S(1)} %collective-permute-done.3.refs_2_, ...), custom_call_target="tpu_custom_call" | custom-call | flops 201326592 | bytes 196608 | tf_op jit(solution)/shard_map/right_products/pallas_call | solution.py:309
Async XLA Ops:
  1.5 11.6 %collective-permute-start = (bf16[1040,128]{1,0:T(8,128)(2,1)S(1)}, bf16[1040,128]{1,0:T(8,128)(2,1)S(1)}, u32[]{:S(2)}, u32[]{:S(2)}) collective-permute-start(bf16[1040,128]{1,0:T(8,128)(2,1)S(1)} %pack_payload.1.payload_ref.refs_0_), channel_id=1, source_target_pairs={{0,1},{1,0},{2,3},{3,2},{4,5},{5,4},{6,7},{7,6},{8,9},{9,8},{10,11... | collective-permute-start | bytes 798728 | tf_op jit(solution)/shard_map/ppermute | solution.py:347
  3.6 12.4 %collective-permute-start.4 = (bf16[1040,128]{1,0:T(8,128)(2,1)S(1)}, bf16[1040,128]{1,0:T(8,128)(2,1)S(1)}, u32[]{:S(2)}, u32[]{:S(2)}) collective-permute-start(bf16[1040,128]{1,0:T(8,128)(2,1)S(1)} %pack_payload.1.payload_ref.refs_0_), channel_id=1, source_target_pairs={{2,5},{3,4},{6,9},{7,8},{10,13},{11,12},{14,17},{15,16},{18,21},{1... | collective-permute-start | bytes 798728 | tf_op jit(solution)/shard_map/ppermute | solution.py:346
  5.6 12.0 %collective-permute-start.2 = (bf16[1040,128]{1,0:T(8,128)(2,1)S(1)}, bf16[1040,128]{1,0:T(8,128)(2,1)S(1)}, u32[]{:S(2)}, u32[]{:S(2)}) collective-permute-start(bf16[1040,128]{1,0:T(8,128)(2,1)S(1)} %pack_payload.1.payload_ref.refs_0_), channel_id=1, source_target_pairs={{0,2},{2,4},{4,6},{6,8},{8,10},{10,12},{12,14},{14,16},{16,18},{18... | collective-permute-start | bytes 798728 | tf_op jit(solution)/shard_map/ppermute | solution.py:348
  5.7 12.0 %collective-permute-start.3 = (bf16[1040,128]{1,0:T(8,128)(2,1)S(1)}, bf16[1040,128]{1,0:T(8,128)(2,1)S(1)}, u32[]{:S(2)}, u32[]{:S(2)}) collective-permute-start(bf16[1040,128]{1,0:T(8,128)(2,1)S(1)} %pack_payload.1.payload_ref.refs_0_), channel_id=1, source_target_pairs={{2,0},{4,2},{6,4},{8,6},{10,8},{12,10},{14,12},{16,14},{18,16},{20... | collective-permute-start | bytes 798728 | tf_op jit(solution)/shard_map/ppermute | solution.py:349
  13.1 4.6 %collective-permute-start.1 = (bf16[1040,128]{1,0:T(8,128)(2,1)S(1)}, bf16[1040,128]{1,0:T(8,128)(2,1)S(1)}, u32[]{:S(2)}, u32[]{:S(2)}) collective-permute-start(bf16[1040,128]{1,0:T(8,128)(2,1)S(1)} %collective-permute-done.refs_1_), channel_id=1, source_target_pairs={{0,2},{2,0},{4,6},{6,4},{8,10},{10,8},{12,14},{14,12},{16,18},{18,... | collective-permute-start | bytes 798728 | tf_op jit(solution)/shard_map/ppermute | solution.py:352

commit v5 on v4

--- a/solution.py
+++ b/solution.py
@@ -22,7 +22,7 @@
 MIB = 1 << 20
 
 
-def pack_kernel(aggregate_hbm, restrict_hbm, out_ref, restrict_ref, wide_ref, aggregate_ref, sems):
+def pack_kernel(aggregate_hbm, restrict_hbm, out_ref, restrict_ref, aggregate_ref, sems):
     rows = pltpu.make_async_copy(restrict_hbm, restrict_ref, sems.at[0])
     tags = pltpu.make_async_copy(aggregate_hbm, aggregate_ref, sems.at[1])
     rows.start()
@@ -36,14 +36,14 @@
         owners = jnp.where(row == p, owner, owners)
     out_ref[TAGS:, :] = owners.astype(jnp.float32).astype(jnp.bfloat16)
     rows.wait()
+    halves = []
     for t in range(BLK // 2):
         x = restrict_ref[:, t * LANES : (t + 1) * LANES].astype(jnp.float32)
         first, second = x[:PAIRS], x[PAIRS:]
-        even = jnp.where(low, first, pltpu.roll(second, BLK, 1))
-        odd = jnp.where(low, pltpu.roll(first, BLK, 1), second)
-        wide_ref[pl.ds(2 * t, PAIRS, stride=BLK), :] = even
-        wide_ref[pl.ds(2 * t + 1, PAIRS, stride=BLK), :] = odd
-    out_ref[:TAGS, :] = wide_ref[...].astype(jnp.bfloat16)
+        halves.append(jnp.where(low, first, pltpu.roll(second, BLK, 1)))
+        halves.append(jnp.where(low, pltpu.roll(first, BLK, 1), second))
+    blocks = jnp.stack(halves, axis=0).swapaxes(0, 1).reshape(TAGS, LANES)
+    out_ref[:TAGS, :] = blocks.astype(jnp.bfloat16)
 
 
 def pack(aggregate, restrict):
@@ -55,7 +55,6 @@
         out_specs=pl.BlockSpec(memory_space=pltpu.VMEM),
         scratch_shapes=[
             pltpu.VMEM(restrict.shape, restrict.dtype),
-            pltpu.VMEM((PAIRS * BLK, LANES), jnp.float32),
             pltpu.SMEM(aggregate.shape, aggregate.dtype),
             pltpu.SemaphoreType.DMA((2,)),
         ],

time: 19.1 us -> 18.8 us (0.984)
  Pallas kernels: 10.3 us -> 9.93 us
    pallas_call x1, Pallas kernels: 1.49 us -> 1.17 us  [pack(): pl.pallas_call(pack_kernel, out_shape=jax.ShapeDtypeStruct((PAYLOAD, LANE...]
where the time goes in v5:
time: 18.8 us; the launch traced here: 18.6 us
  Pallas kernels  9.93 us (53%)
  starting transfers between devices  7.65 us (41%)
  waiting for transfers between devices  0.99 us (5%)
    pallas_call x1, Pallas kernels, left_sums(): pl.pallas_call(functools.partial(left_kernel, order), out_shape=jax.Shape...  6.89 us
    ppermute x1, starting transfers between devices, paired_plan(): inner = lax.ppermute(beside, 'rows', evens)  3.02 us
    ppermute x1, starting transfers between devices, paired_plan(): beside = lax.ppermute(payload, 'cols', across)  2.13 us
    ppermute x1, starting transfers between devices, paired_plan(): far = lax.ppermute(payload, ('rows', 'cols'), crossed)  1.99 us
    pallas_call x1, Pallas kernels, right_products(): pl.pallas_call(functools.partial(right_kernel, sources, order, first), ou...  1.29 us
    pallas_call x1, Pallas kernels, pack(): pl.pallas_call(pack_kernel, out_shape=jax.ShapeDtypeStruct((PAYLOAD, LANE...  1.17 us
    ppermute x1, waiting for transfers between devices, paired_plan(): below = lax.ppermute(payload, 'rows', ring)  0.98 us
    pallas_call x1, Pallas kernels, near_products(): pl.pallas_call(functools.partial(near_kernel, first), out_shape=jax.Shape...  0.58 us
  transfers between devices with their start and end apart: 5, of which 1 were waited for; matrix products, arithmetic and copies ran while one was open for 0% of the time, Pallas kernels for 40%

profile of v5, /device:TPU:1, one launch (start us, length us, event | category | flops | bytes accessed | tf_op | source)
XLA Modules:
  0.0 18.6 jit_solution(14936804965387751771)
XLA Ops:
  0.0 1.2 %pack_payload.1.payload_ref.refs_0_ = bf16[1040,128]{1,0:T(8,128)(2,1)S(1)} custom-call(s32[32]{0:T(128)} %aggregate_hbm.3, bf16[32,4096]{1,0:T(8,128)(2,1)} %restrict_hbm.1), custom_call_target="tpu_custom_call" | custom-call | tf_op jit(solution)/shard_map/pack_payload/pallas_call | solution.py:51
  1.2 2.1 %collective-permute-start = (bf16[1040,128]{1,0:T(8,128)(2,1)S(1)}, bf16[1040,128]{1,0:T(8,128)(2,1)S(1)}, u32[]{:S(2)}, u32[]{:S(2)}) collective-permute-start(bf16[1040,128]{1,0:T(8,128)(2,1)S(1)} %pack_payload.1.payload_ref.refs_0_), channel_id=1, source_target_pairs={{0,1},{1,0},{2,3},{3,2},{4,5},{5,4},{6,7},{7,6},{8,9},{9,8},{10,11... | collective-permute-start | bytes 798728 | tf_op jit(solution)/shard_map/ppermute | solution.py:346
  3.3 2.0 %collective-permute-start.4 = (bf16[1040,128]{1,0:T(8,128)(2,1)S(1)}, bf16[1040,128]{1,0:T(8,128)(2,1)S(1)}, u32[]{:S(2)}, u32[]{:S(2)}) collective-permute-start(bf16[1040,128]{1,0:T(8,128)(2,1)S(1)} %pack_payload.1.payload_ref.refs_0_), channel_id=1, source_target_pairs={{2,5},{3,4},{6,9},{7,8},{10,13},{11,12},{14,17},{15,16},{18,21},{1... | collective-permute-start | bytes 798728 | tf_op jit(solution)/shard_map/ppermute | solution.py:345
  5.3 0.1 collective-permute-start.2
  5.4 0.5 %collective-permute-start.3 = (bf16[1040,128]{1,0:T(8,128)(2,1)S(1)}, bf16[1040,128]{1,0:T(8,128)(2,1)S(1)}, u32[]{:S(2)}, u32[]{:S(2)}) collective-permute-start(bf16[1040,128]{1,0:T(8,128)(2,1)S(1)} %pack_payload.1.payload_ref.refs_0_), channel_id=1, source_target_pairs={{2,0},{4,2},{6,4},{8,6},{10,8},{12,10},{14,12},{16,14},{18,16},{20... | collective-permute-start | bytes 798728 | tf_op jit(solution)/shard_map/ppermute | solution.py:348
  5.8 6.9 %left_sums.1.lefts_ref = bf16[6,128,2048]{2,1,0:T(8,128)(2,1)S(1)} custom-call(s32[32,27]{1,0:T(8,128)} %columns_hbm.1, s32[32]{0:T(128)} %counts_hbm.1, s32[32]{0:T(128)} %aggregate_hbm.3, bf16[1040,128]{1,0:T(8,128)(2,1)S(1)} %pack_payload.1.payload_ref.refs_0_, bf16[2,16,64,1728]{3,2,1,0:T(8,128)(2,1)} %bitcast.1), custom_call_target="tpu_custom_call" | custom-call | flops 905969664 | bytes 2097152 | tf_op jit(solution)/shard_map/left_sums/pallas_call | solution.py:204
  12.7 0.0 collective-permute-done.refs_1_
  12.7 3.0 %collective-permute-start.1 = (bf16[1040,128]{1,0:T(8,128)(2,1)S(1)}, bf16[1040,128]{1,0:T(8,128)(2,1)S(1)}, u32[]{:S(2)}, u32[]{:S(2)}) collective-permute-start(bf16[1040,128]{1,0:T(8,128)(2,1)S(1)} %collective-permute-done.refs_1_), channel_id=1, source_target_pairs={{0,2},{2,0},{4,6},{6,4},{8,10},{10,8},{12,14},{14,12},{16,18},{18,... | collective-permute-start | bytes 798728 | tf_op jit(solution)/shard_map/ppermute | solution.py:351
  15.8 0.0 collective-permute-done.4.refs_2_
  15.8 0.6 %near_products.1.refs_3_ = f32[3,2,64,128]{3,2,1,0:T(8,128)S(1)} custom-call(bf16[6,128,2048]{2,1,0:T(8,128)(2,1)S(1)} %left_sums.1.lefts_ref, bf16[1040,128]{1,0:T(8,128)(2,1)S(1)} %pack_payload.1.payload_ref.refs_0_, bf16[1040,128]{1,0:T(8,128)(2,1)S(1)} %collective-permute-done.refs_1_, bf16[1040,128]{1,0:T(8,128)(2,1)S(1)} %collective-permute-done.4.refs_2_), custom_call_target="tpu_custom_call" | custom-call | flops 201326592 | bytes 196608 | tf_op jit(solution)/shard_map/near_products/pallas_call | solution.py:259
  16.3 1.0 %collective-permute-done.2.refs_1_ = bf16[1040,128]{1,0:T(8,128)(2,1)S(1)} collective-permute-done((bf16[1040,128]{1,0:T(8,128)(2,1)S(1)}, bf16[1040,128]{1,0:T(8,128)(2,1)S(1)}, u32[]{:S(2)}, u32[]{:S(2)}) %collective-permute-start.2) | collective-permute-done | bytes 266272 | tf_op jit(solution)/shard_map/ppermute | solution.py:347
  17.3 0.0 collective-permute-done.3.refs_2_
  17.3 0.0 collective-permute-done.1.refs_0_
  17.3 1.3 %right_products.1 = f32[2,64,768]{2,1,0:T(8,128)} custom-call(bf16[6,128,2048]{2,1,0:T(8,128)(2,1)S(1)} %left_sums.1.lefts_ref, bf16[1040,128]{1,0:T(8,128)(2,1)S(1)} %collective-permute-done.1.refs_0_, bf16[1040,128]{1,0:T(8,128)(2,1)S(1)} %collective-permute-done.2.refs_1_, bf16[1040,128]{1,0:T(8,128)(2,1)S(1)} %collective-permute-done.3.refs_2_, ...), custom_call_target="tpu_custom_call" | custom-call | flops 201326592 | bytes 196608 | tf_op jit(solution)/shard_map/right_products/pallas_call | solution.py:308
Async XLA Ops:
  1.2 11.5 %collective-permute-start = (bf16[1040,128]{1,0:T(8,128)(2,1)S(1)}, bf16[1040,128]{1,0:T(8,128)(2,1)S(1)}, u32[]{:S(2)}, u32[]{:S(2)}) collective-permute-start(bf16[1040,128]{1,0:T(8,128)(2,1)S(1)} %pack_payload.1.payload_ref.refs_0_), channel_id=1, source_target_pairs={{0,1},{1,0},{2,3},{3,2},{4,5},{5,4},{6,7},{7,6},{8,9},{9,8},{10,11... | collective-permute-start | bytes 798728 | tf_op jit(solution)/shard_map/ppermute | solution.py:346
  3.3 12.4 %collective-permute-start.4 = (bf16[1040,128]{1,0:T(8,128)(2,1)S(1)}, bf16[1040,128]{1,0:T(8,128)(2,1)S(1)}, u32[]{:S(2)}, u32[]{:S(2)}) collective-permute-start(bf16[1040,128]{1,0:T(8,128)(2,1)S(1)} %pack_payload.1.payload_ref.refs_0_), channel_id=1, source_target_pairs={{2,5},{3,4},{6,9},{7,8},{10,13},{11,12},{14,17},{15,16},{18,21},{1... | collective-permute-start | bytes 798728 | tf_op jit(solution)/shard_map/ppermute | solution.py:345
  5.3 12.0 %collective-permute-start.2 = (bf16[1040,128]{1,0:T(8,128)(2,1)S(1)}, bf16[1040,128]{1,0:T(8,128)(2,1)S(1)}, u32[]{:S(2)}, u32[]{:S(2)}) collective-permute-start(bf16[1040,128]{1,0:T(8,128)(2,1)S(1)} %pack_payload.1.payload_ref.refs_0_), channel_id=1, source_target_pairs={{0,2},{2,4},{4,6},{6,8},{8,10},{10,12},{12,14},{14,16},{16,18},{18... | collective-permute-start | bytes 798728 | tf_op jit(solution)/shard_map/ppermute | solution.py:347
  5.4 12.0 %collective-permute-start.3 = (bf16[1040,128]{1,0:T(8,128)(2,1)S(1)}, bf16[1040,128]{1,0:T(8,128)(2,1)S(1)}, u32[]{:S(2)}, u32[]{:S(2)}) collective-permute-start(bf16[1040,128]{1,0:T(8,128)(2,1)S(1)} %pack_payload.1.payload_ref.refs_0_), channel_id=1, source_target_pairs={{2,0},{4,2},{6,4},{8,6},{10,8},{12,10},{14,12},{16,14},{18,16},{20... | collective-permute-start | bytes 798728 | tf_op jit(solution)/shard_map/ppermute | solution.py:348
  12.7 4.6 %collective-permute-start.1 = (bf16[1040,128]{1,0:T(8,128)(2,1)S(1)}, bf16[1040,128]{1,0:T(8,128)(2,1)S(1)}, u32[]{:S(2)}, u32[]{:S(2)}) collective-permute-start(bf16[1040,128]{1,0:T(8,128)(2,1)S(1)} %collective-permute-done.refs_1_), channel_id=1, source_target_pairs={{0,2},{2,0},{4,6},{6,4},{8,10},{10,8},{12,14},{14,12},{16,18},{18,... | collective-permute-start | bytes 798728 | tf_op jit(solution)/shard_map/ppermute | solution.py:351

commit v6 on v5

--- a/solution.py
+++ b/solution.py
@@ -336,10 +336,10 @@
         return [
             (2 + c, None),
             (3 - c, None),
+            (4 + c, high),
+            (c, low),
+            (4 * up + 1 - c, None),
             (4 - 4 * up + 1 - c, far),
-            (4 * up + 1 - c, None),
-            (c, low),
-            (4 + c, high),
         ]
 
     far = lax.ppermute(payload, ("rows", "cols"), crossed)
@@ -349,9 +349,9 @@
     lefts = left_sums(columns, counts, aggregate, payload, matrix_blocks, 6, order)
     lefts, beside = lax.optimization_barrier((lefts, beside))
     inner = lax.ppermute(beside, "rows", evens)
-    near = near_products(lefts, [payload, beside, far], 0)
-    sources = [(index, 0) for index in range(3)]
-    return right_products(lefts, [inner, below, above], sources, order, 6 * LANES, near)
+    near = near_products(lefts, [payload, beside, above, below], 0)
+    sources = [(index, 0) for index in range(2)]
+    return right_products(lefts, [inner, far], sources, order, 6 * LANES, near)
 
 
 def general_plan(columns, counts, aggregate, matrix_blocks, payload, row_count, col_count):

time: 18.8 us -> 18.6 us (0.989)
  starting transfers between devices: 7.65 us -> 7.35 us
    ppermute x1, starting transfers between devices: 1.99 us -> 0.45 us  [paired_plan(): far = lax.ppermute(payload, ('rows', 'cols'), crossed)]
    ppermute x1, waiting for transfers between devices: 0.01 us -> 1.12 us  [paired_plan(): far = lax.ppermute(payload, ('rows', 'cols'), crossed)]
    ppermute x1, starting transfers between devices: 0.06 us -> 1.1 us  [paired_plan(): below = lax.ppermute(payload, 'rows', ring)]
    ppermute x1, waiting for transfers between devices: 0.98 us -> 0.01 us  [paired_plan(): below = lax.ppermute(payload, 'rows', ring)]
    ppermute x1, starting transfers between devices: 0.45 us -> 0.96 us  [paired_plan(): above = lax.ppermute(payload, 'rows', [(b, a) for a, b in ring])]
    ppermute x1, starting transfers between devices: 3.02 us -> 2.71 us  [paired_plan(): inner = lax.ppermute(beside, 'rows', evens)]
  transfers between devices with their start and end apart: 5 -> 5, of which waited for: 1 -> 1; matrix products, arithmetic and copies ran while one was open for 0% -> 0% of each run, Pallas kernels for 40% -> 41%
where the time goes in v6:
time: 18.6 us; the launch traced here: 18.5 us
  Pallas kernels  9.94 us (53%)
  starting transfers between devices  7.35 us (40%)
  waiting for transfers between devices  1.13 us (6%)
    pallas_call x1, Pallas kernels, left_sums(): pl.pallas_call(functools.partial(left_kernel, order), out_shape=jax.Shape...  6.88 us
    ppermute x1, starting transfers between devices, paired_plan(): inner = lax.ppermute(beside, 'rows', evens)  2.71 us
    ppermute x1, starting transfers between devices, paired_plan(): beside = lax.ppermute(payload, 'cols', across)  2.13 us
    pallas_call x1, Pallas kernels, pack(): pl.pallas_call(pack_kernel, out_shape=jax.ShapeDtypeStruct((PAYLOAD, LANE...  1.17 us
    pallas_call x1, Pallas kernels, right_products(): pl.pallas_call(functools.partial(right_kernel, sources, order, first), ou...  1.16 us
    ppermute x1, waiting for transfers between devices, paired_plan(): far = lax.ppermute(payload, ('rows', 'cols'), crossed)  1.12 us
    ppermute x1, starting transfers between devices, paired_plan(): below = lax.ppermute(payload, 'rows', ring)  1.1 us
    ppermute x1, starting transfers between devices, paired_plan(): above = lax.ppermute(payload, 'rows', [(b, a) for a, b in ring])  0.96 us
  transfers between devices with their start and end apart: 5, of which 1 were waited for; matrix products, arithmetic and copies ran while one was open for 0% of the time, Pallas kernels for 41%

profile of v6, /device:TPU:1, one launch (start us, length us, event | category | flops | bytes accessed | tf_op | source)
XLA Modules:
  0.0 18.5 jit_solution(937634329024461470)
XLA Ops:
  0.0 1.2 %pack_payload.1.payload_ref.refs_0_ = bf16[1040,128]{1,0:T(8,128)(2,1)S(1)} custom-call(s32[32]{0:T(128)} %aggregate_hbm.3, bf16[32,4096]{1,0:T(8,128)(2,1)} %restrict_hbm.1), custom_call_target="tpu_custom_call" | custom-call | tf_op jit(solution)/shard_map/pack_payload/pallas_call | solution.py:51
  1.2 2.1 %collective-permute-start = (bf16[1040,128]{1,0:T(8,128)(2,1)S(1)}, bf16[1040,128]{1,0:T(8,128)(2,1)S(1)}, u32[]{:S(2)}, u32[]{:S(2)}) collective-permute-start(bf16[1040,128]{1,0:T(8,128)(2,1)S(1)} %pack_payload.1.payload_ref.refs_0_), channel_id=1, source_target_pairs={{0,1},{1,0},{2,3},{3,2},{4,5},{5,4},{6,7},{7,6},{8,9},{9,8},{10,11... | collective-permute-start | bytes 798728 | tf_op jit(solution)/shard_map/ppermute | solution.py:346
  3.3 1.0 %collective-permute-start.3 = (bf16[1040,128]{1,0:T(8,128)(2,1)S(1)}, bf16[1040,128]{1,0:T(8,128)(2,1)S(1)}, u32[]{:S(2)}, u32[]{:S(2)}) collective-permute-start(bf16[1040,128]{1,0:T(8,128)(2,1)S(1)} %pack_payload.1.payload_ref.refs_0_), channel_id=1, source_target_pairs={{2,0},{4,2},{6,4},{8,6},{10,8},{12,10},{14,12},{16,14},{18,16},{20... | collective-permute-start | bytes 798728 | tf_op jit(solution)/shard_map/ppermute | solution.py:348
  4.3 1.1 %collective-permute-start.4 = (bf16[1040,128]{1,0:T(8,128)(2,1)S(1)}, bf16[1040,128]{1,0:T(8,128)(2,1)S(1)}, u32[]{:S(2)}, u32[]{:S(2)}) collective-permute-start(bf16[1040,128]{1,0:T(8,128)(2,1)S(1)} %pack_payload.1.payload_ref.refs_0_), channel_id=1, source_target_pairs={{0,2},{2,4},{4,6},{6,8},{8,10},{10,12},{12,14},{14,16},{16,18},{18... | collective-permute-start | bytes 798728 | tf_op jit(solution)/shard_map/ppermute | solution.py:347
  5.4 0.5 %collective-permute-start.2 = (bf16[1040,128]{1,0:T(8,128)(2,1)S(1)}, bf16[1040,128]{1,0:T(8,128)(2,1)S(1)}, u32[]{:S(2)}, u32[]{:S(2)}) collective-permute-start(bf16[1040,128]{1,0:T(8,128)(2,1)S(1)} %pack_payload.1.payload_ref.refs_0_), channel_id=1, source_target_pairs={{2,5},{3,4},{6,9},{7,8},{10,13},{11,12},{14,17},{15,16},{18,21},{1... | collective-permute-start | bytes 798728 | tf_op jit(solution)/shard_map/ppermute | solution.py:345
  5.8 6.9 %left_sums.1.lefts_ref = bf16[6,128,2048]{2,1,0:T(8,128)(2,1)S(1)} custom-call(s32[32,27]{1,0:T(8,128)} %columns_hbm.1, s32[32]{0:T(128)} %counts_hbm.1, s32[32]{0:T(128)} %aggregate_hbm.3, bf16[1040,128]{1,0:T(8,128)(2,1)S(1)} %pack_payload.1.payload_ref.refs_0_, bf16[2,16,64,1728]{3,2,1,0:T(8,128)(2,1)} %bitcast.1), custom_call_target="tpu_custom_call" | custom-call | flops 905969664 | bytes 2097152 | tf_op jit(solution)/shard_map/left_sums/pallas_call | solution.py:204
  12.7 0.0 collective-permute-done.refs_1_
  12.7 2.7 %collective-permute-start.1 = (bf16[1040,128]{1,0:T(8,128)(2,1)S(1)}, bf16[1040,128]{1,0:T(8,128)(2,1)S(1)}, u32[]{:S(2)}, u32[]{:S(2)}) collective-permute-start(bf16[1040,128]{1,0:T(8,128)(2,1)S(1)} %collective-permute-done.refs_1_), channel_id=1, source_target_pairs={{0,2},{2,0},{4,6},{6,4},{8,10},{10,8},{12,14},{14,12},{16,18},{18,... | collective-permute-start | bytes 798728 | tf_op jit(solution)/shard_map/ppermute | solution.py:351
  15.4 0.0 collective-permute-done.3.refs_2_
  15.4 0.0 collective-permute-done.4.refs_3_
  15.4 0.7 %near_products.1.refs_2_ = f32[4,2,64,128]{3,2,1,0:T(8,128)S(1)} custom-call(bf16[6,128,2048]{2,1,0:T(8,128)(2,1)S(1)} %left_sums.1.lefts_ref, bf16[1040,128]{1,0:T(8,128)(2,1)S(1)} %pack_payload.1.payload_ref.refs_0_, bf16[1040,128]{1,0:T(8,128)(2,1)S(1)} %collective-permute-done.refs_1_, bf16[1040,128]{1,0:T(8,128)(2,1)S(1)} %collective-permute-done.3.refs_2_, ...), custom_call_target="tpu_custom_call" | custom-call | flops 268435456 | bytes 262144 | tf_op jit(solution)/shard_map/near_products/pallas_call | solution.py:259
  16.2 1.1 %collective-permute-done.2.refs_1_ = bf16[1040,128]{1,0:T(8,128)(2,1)S(1)} collective-permute-done((bf16[1040,128]{1,0:T(8,128)(2,1)S(1)}, bf16[1040,128]{1,0:T(8,128)(2,1)S(1)}, u32[]{:S(2)}, u32[]{:S(2)}) %collective-permute-start.2) | collective-permute-done | bytes 266272 | tf_op jit(solution)/shard_map/ppermute | solution.py:345
  17.3 0.0 collective-permute-done.1.refs_0_
  17.3 1.2 %right_products.1 = f32[2,64,768]{2,1,0:T(8,128)} custom-call(bf16[6,128,2048]{2,1,0:T(8,128)(2,1)S(1)} %left_sums.1.lefts_ref, bf16[1040,128]{1,0:T(8,128)(2,1)S(1)} %collective-permute-done.1.refs_0_, bf16[1040,128]{1,0:T(8,128)(2,1)S(1)} %collective-permute-done.2.refs_1_, f32[4,2,64,128]{3,2,1,0:T(8,128)S(1)} %near_products.1.refs_2_), custom_call_target="tpu_custom_call" | custom-call | flops 134217728 | bytes 131072 | tf_op jit(solution)/shard_map/right_products/pallas_call | solution.py:308
Async XLA Ops:
  1.2 11.5 %collective-permute-start = (bf16[1040,128]{1,0:T(8,128)(2,1)S(1)}, bf16[1040,128]{1,0:T(8,128)(2,1)S(1)}, u32[]{:S(2)}, u32[]{:S(2)}) collective-permute-start(bf16[1040,128]{1,0:T(8,128)(2,1)S(1)} %pack_payload.1.payload_ref.refs_0_), channel_id=1, source_target_pairs={{0,1},{1,0},{2,3},{3,2},{4,5},{5,4},{6,7},{7,6},{8,9},{9,8},{10,11... | collective-permute-start | bytes 798728 | tf_op jit(solution)/shard_map/ppermute | solution.py:346
  3.3 12.1 %collective-permute-start.3 = (bf16[1040,128]{1,0:T(8,128)(2,1)S(1)}, bf16[1040,128]{1,0:T(8,128)(2,1)S(1)}, u32[]{:S(2)}, u32[]{:S(2)}) collective-permute-start(bf16[1040,128]{1,0:T(8,128)(2,1)S(1)} %pack_payload.1.payload_ref.refs_0_), channel_id=1, source_target_pairs={{2,0},{4,2},{6,4},{8,6},{10,8},{12,10},{14,12},{16,14},{18,16},{20... | collective-permute-start | bytes 798728 | tf_op jit(solution)/shard_map/ppermute | solution.py:348
  4.3 11.2 %collective-permute-start.4 = (bf16[1040,128]{1,0:T(8,128)(2,1)S(1)}, bf16[1040,128]{1,0:T(8,128)(2,1)S(1)}, u32[]{:S(2)}, u32[]{:S(2)}) collective-permute-start(bf16[1040,128]{1,0:T(8,128)(2,1)S(1)} %pack_payload.1.payload_ref.refs_0_), channel_id=1, source_target_pairs={{0,2},{2,4},{4,6},{6,8},{8,10},{10,12},{12,14},{14,16},{16,18},{18... | collective-permute-start | bytes 798728 | tf_op jit(solution)/shard_map/ppermute | solution.py:347
  5.4 11.9 %collective-permute-start.2 = (bf16[1040,128]{1,0:T(8,128)(2,1)S(1)}, bf16[1040,128]{1,0:T(8,128)(2,1)S(1)}, u32[]{:S(2)}, u32[]{:S(2)}) collective-permute-start(bf16[1040,128]{1,0:T(8,128)(2,1)S(1)} %pack_payload.1.payload_ref.refs_0_), channel_id=1, source_target_pairs={{2,5},{3,4},{6,9},{7,8},{10,13},{11,12},{14,17},{15,16},{18,21},{1... | collective-permute-start | bytes 798728 | tf_op jit(solution)/shard_map/ppermute | solution.py:345
  12.7 4.6 %collective-permute-start.1 = (bf16[1040,128]{1,0:T(8,128)(2,1)S(1)}, bf16[1040,128]{1,0:T(8,128)(2,1)S(1)}, u32[]{:S(2)}, u32[]{:S(2)}) collective-permute-start(bf16[1040,128]{1,0:T(8,128)(2,1)S(1)} %collective-permute-done.refs_1_), channel_id=1, source_target_pairs={{0,2},{2,0},{4,6},{6,4},{8,10},{10,8},{12,14},{14,12},{16,18},{18,... | collective-permute-start | bytes 798728 | tf_op jit(solution)/shard_map/ppermute | solution.py:351

commit v7 on v6

--- a/solution.py
+++ b/solution.py
@@ -347,7 +347,7 @@
     below = lax.ppermute(payload, "rows", ring)
     above = lax.ppermute(payload, "rows", [(b, a) for a, b in ring])
     lefts = left_sums(columns, counts, aggregate, payload, matrix_blocks, 6, order)
-    lefts, beside = lax.optimization_barrier((lefts, beside))
+    lefts, beside, above = lax.optimization_barrier((lefts, beside, above))
     inner = lax.ppermute(beside, "rows", evens)
     near = near_products(lefts, [payload, beside, above, below], 0)
     sources = [(index, 0) for index in range(2)]

time: 18.6 us -> 18.6 us (level)
  no operation moved by 1% of the time
where the time goes in v7:
time: 18.6 us; the launch traced here: 18.5 us
  Pallas kernels  9.96 us (54%)
  starting transfers between devices  7.33 us (39%)
  waiting for transfers between devices  1.12 us (6%)
    pallas_call x1, Pallas kernels, left_sums(): pl.pallas_call(functools.partial(left_kernel, order), out_shape=jax.Shape...  6.89 us
    ppermute x1, starting transfers between devices, paired_plan(): inner = lax.ppermute(beside, 'rows', evens)  2.7 us
    ppermute x1, starting transfers between devices, paired_plan(): beside = lax.ppermute(payload, 'cols', across)  2.13 us
    pallas_call x1, Pallas kernels, pack(): pl.pallas_call(pack_kernel, out_shape=jax.ShapeDtypeStruct((PAYLOAD, LANE...  1.17 us
    pallas_call x1, Pallas kernels, right_products(): pl.pallas_call(functools.partial(right_kernel, sources, order, first), ou...  1.16 us
    ppermute x1, waiting for transfers between devices, paired_plan(): far = lax.ppermute(payload, ('rows', 'cols'), crossed)  1.11 us
    ppermute x1, starting transfers between devices, paired_plan(): below = lax.ppermute(payload, 'rows', ring)  1.1 us
    ppermute x1, starting transfers between devices, paired_plan(): above = lax.ppermute(payload, 'rows', [(b, a) for a, b in ring])  0.96 us
  transfers between devices with their start and end apart: 5, of which 1 were waited for; matrix products, arithmetic and copies ran while one was open for 0% of the time, Pallas kernels for 41%

profile of v7, /device:TPU:1, one launch (start us, length us, event | category | flops | bytes accessed | tf_op | source)
XLA Modules:
  0.0 18.5 jit_solution(18299446861869330389)
XLA Ops:
  0.0 1.2 %pack_payload.1.payload_ref.refs_0_ = bf16[1040,128]{1,0:T(8,128)(2,1)S(1)} custom-call(s32[32]{0:T(128)} %aggregate_hbm.3, bf16[32,4096]{1,0:T(8,128)(2,1)} %restrict_hbm.1), custom_call_target="tpu_custom_call" | custom-call | tf_op jit(solution)/shard_map/pack_payload/pallas_call | solution.py:51
  1.2 2.1 %collective-permute-start = (bf16[1040,128]{1,0:T(8,128)(2,1)S(1)}, bf16[1040,128]{1,0:T(8,128)(2,1)S(1)}, u32[]{:S(2)}, u32[]{:S(2)}) collective-permute-start(bf16[1040,128]{1,0:T(8,128)(2,1)S(1)} %pack_payload.1.payload_ref.refs_0_), channel_id=1, source_target_pairs={{0,1},{1,0},{2,3},{3,2},{4,5},{5,4},{6,7},{7,6},{8,9},{9,8},{10,11... | collective-permute-start | bytes 798728 | tf_op jit(solution)/shard_map/ppermute | solution.py:346
  3.3 1.0 %collective-permute-start.1 = (bf16[1040,128]{1,0:T(8,128)(2,1)S(1)}, bf16[1040,128]{1,0:T(8,128)(2,1)S(1)}, u32[]{:S(2)}, u32[]{:S(2)}) collective-permute-start(bf16[1040,128]{1,0:T(8,128)(2,1)S(1)} %pack_payload.1.payload_ref.refs_0_), channel_id=1, source_target_pairs={{2,0},{4,2},{6,4},{8,6},{10,8},{12,10},{14,12},{16,14},{18,16},{20... | collective-permute-start | bytes 798728 | tf_op jit(solution)/shard_map/ppermute | solution.py:348
  4.3 1.1 %collective-permute-start.4 = (bf16[1040,128]{1,0:T(8,128)(2,1)S(1)}, bf16[1040,128]{1,0:T(8,128)(2,1)S(1)}, u32[]{:S(2)}, u32[]{:S(2)}) collective-permute-start(bf16[1040,128]{1,0:T(8,128)(2,1)S(1)} %pack_payload.1.payload_ref.refs_0_), channel_id=1, source_target_pairs={{0,2},{2,4},{4,6},{6,8},{8,10},{10,12},{12,14},{14,16},{16,18},{18... | collective-permute-start | bytes 798728 | tf_op jit(solution)/shard_map/ppermute | solution.py:347
  5.4 0.5 %collective-permute-start.3 = (bf16[1040,128]{1,0:T(8,128)(2,1)S(1)}, bf16[1040,128]{1,0:T(8,128)(2,1)S(1)}, u32[]{:S(2)}, u32[]{:S(2)}) collective-permute-start(bf16[1040,128]{1,0:T(8,128)(2,1)S(1)} %pack_payload.1.payload_ref.refs_0_), channel_id=1, source_target_pairs={{2,5},{3,4},{6,9},{7,8},{10,13},{11,12},{14,17},{15,16},{18,21},{1... | collective-permute-start | bytes 798728 | tf_op jit(solution)/shard_map/ppermute | solution.py:345
  5.8 6.9 %left_sums.1.lefts_ref = bf16[6,128,2048]{2,1,0:T(8,128)(2,1)S(1)} custom-call(s32[32,27]{1,0:T(8,128)} %columns_hbm.1, s32[32]{0:T(128)} %counts_hbm.1, s32[32]{0:T(128)} %aggregate_hbm.3, bf16[1040,128]{1,0:T(8,128)(2,1)S(1)} %pack_payload.1.payload_ref.refs_0_, bf16[2,16,64,1728]{3,2,1,0:T(8,128)(2,1)} %bitcast.1), custom_call_target="tpu_custom_call" | custom-call | flops 905969664 | bytes 2097152 | tf_op jit(solution)/shard_map/left_sums/pallas_call | solution.py:204
  12.7 0.0 collective-permute-done.refs_1_
  12.7 0.0 collective-permute-done.1.refs_2_
  12.7 2.7 %collective-permute-start.2 = (bf16[1040,128]{1,0:T(8,128)(2,1)S(1)}, bf16[1040,128]{1,0:T(8,128)(2,1)S(1)}, u32[]{:S(2)}, u32[]{:S(2)}) collective-permute-start(bf16[1040,128]{1,0:T(8,128)(2,1)S(1)} %collective-permute-done.refs_1_), channel_id=1, source_target_pairs={{0,2},{2,0},{4,6},{6,4},{8,10},{10,8},{12,14},{14,12},{16,18},{18,... | collective-permute-start | bytes 798728 | tf_op jit(solution)/shard_map/ppermute | solution.py:351
  15.4 0.0 collective-permute-done.4.refs_3_
  15.4 0.7 %near_products.1.refs_2_ = f32[4,2,64,128]{3,2,1,0:T(8,128)S(1)} custom-call(bf16[6,128,2048]{2,1,0:T(8,128)(2,1)S(1)} %left_sums.1.lefts_ref, bf16[1040,128]{1,0:T(8,128)(2,1)S(1)} %pack_payload.1.payload_ref.refs_0_, bf16[1040,128]{1,0:T(8,128)(2,1)S(1)} %collective-permute-done.refs_1_, bf16[1040,128]{1,0:T(8,128)(2,1)S(1)} %collective-permute-done.1.refs_2_, ...), custom_call_target="tpu_custom_call" | custom-call | flops 268435456 | bytes 262144 | tf_op jit(solution)/shard_map/near_products/pallas_call | solution.py:259
  16.2 1.1 %collective-permute-done.3.refs_1_ = bf16[1040,128]{1,0:T(8,128)(2,1)S(1)} collective-permute-done((bf16[1040,128]{1,0:T(8,128)(2,1)S(1)}, bf16[1040,128]{1,0:T(8,128)(2,1)S(1)}, u32[]{:S(2)}, u32[]{:S(2)}) %collective-permute-start.3) | collective-permute-done | bytes 266272 | tf_op jit(solution)/shard_map/ppermute | solution.py:345
  17.3 0.0 collective-permute-done.2.refs_0_
  17.3 1.2 %right_products.1 = f32[2,64,768]{2,1,0:T(8,128)} custom-call(bf16[6,128,2048]{2,1,0:T(8,128)(2,1)S(1)} %left_sums.1.lefts_ref, bf16[1040,128]{1,0:T(8,128)(2,1)S(1)} %collective-permute-done.2.refs_0_, bf16[1040,128]{1,0:T(8,128)(2,1)S(1)} %collective-permute-done.3.refs_1_, f32[4,2,64,128]{3,2,1,0:T(8,128)S(1)} %near_products.1.refs_2_), custom_call_target="tpu_custom_call" | custom-call | flops 134217728 | bytes 131072 | tf_op jit(solution)/shard_map/right_products/pallas_call | solution.py:308
Async XLA Ops:
  1.2 11.5 %collective-permute-start = (bf16[1040,128]{1,0:T(8,128)(2,1)S(1)}, bf16[1040,128]{1,0:T(8,128)(2,1)S(1)}, u32[]{:S(2)}, u32[]{:S(2)}) collective-permute-start(bf16[1040,128]{1,0:T(8,128)(2,1)S(1)} %pack_payload.1.payload_ref.refs_0_), channel_id=1, source_target_pairs={{0,1},{1,0},{2,3},{3,2},{4,5},{5,4},{6,7},{7,6},{8,9},{9,8},{10,11... | collective-permute-start | bytes 798728 | tf_op jit(solution)/shard_map/ppermute | solution.py:346
  3.3 9.4 %collective-permute-start.1 = (bf16[1040,128]{1,0:T(8,128)(2,1)S(1)}, bf16[1040,128]{1,0:T(8,128)(2,1)S(1)}, u32[]{:S(2)}, u32[]{:S(2)}) collective-permute-start(bf16[1040,128]{1,0:T(8,128)(2,1)S(1)} %pack_payload.1.payload_ref.refs_0_), channel_id=1, source_target_pairs={{2,0},{4,2},{6,4},{8,6},{10,8},{12,10},{14,12},{16,14},{18,16},{20... | collective-permute-start | bytes 798728 | tf_op jit(solution)/shard_map/ppermute | solution.py:348
  4.3 11.2 %collective-permute-start.4 = (bf16[1040,128]{1,0:T(8,128)(2,1)S(1)}, bf16[1040,128]{1,0:T(8,128)(2,1)S(1)}, u32[]{:S(2)}, u32[]{:S(2)}) collective-permute-start(bf16[1040,128]{1,0:T(8,128)(2,1)S(1)} %pack_payload.1.payload_ref.refs_0_), channel_id=1, source_target_pairs={{0,2},{2,4},{4,6},{6,8},{8,10},{10,12},{12,14},{14,16},{16,18},{18... | collective-permute-start | bytes 798728 | tf_op jit(solution)/shard_map/ppermute | solution.py:347
  5.4 11.9 %collective-permute-start.3 = (bf16[1040,128]{1,0:T(8,128)(2,1)S(1)}, bf16[1040,128]{1,0:T(8,128)(2,1)S(1)}, u32[]{:S(2)}, u32[]{:S(2)}) collective-permute-start(bf16[1040,128]{1,0:T(8,128)(2,1)S(1)} %pack_payload.1.payload_ref.refs_0_), channel_id=1, source_target_pairs={{2,5},{3,4},{6,9},{7,8},{10,13},{11,12},{14,17},{15,16},{18,21},{1... | collective-permute-start | bytes 798728 | tf_op jit(solution)/shard_map/ppermute | solution.py:345
  12.7 4.5 %collective-permute-start.2 = (bf16[1040,128]{1,0:T(8,128)(2,1)S(1)}, bf16[1040,128]{1,0:T(8,128)(2,1)S(1)}, u32[]{:S(2)}, u32[]{:S(2)}) collective-permute-start(bf16[1040,128]{1,0:T(8,128)(2,1)S(1)} %collective-permute-done.refs_1_), channel_id=1, source_target_pairs={{0,2},{2,0},{4,6},{6,4},{8,10},{10,8},{12,14},{14,12},{16,18},{18,... | collective-permute-start | bytes 798728 | tf_op jit(solution)/shard_map/ppermute | solution.py:351

commit v8 on v6

--- a/solution.py
+++ b/solution.py
@@ -338,8 +338,8 @@
             (3 - c, None),
             (4 + c, high),
             (c, low),
+            (4 - 4 * up + 1 - c, far),
             (4 * up + 1 - c, None),
-            (4 - 4 * up + 1 - c, far),
         ]
 
     far = lax.ppermute(payload, ("rows", "cols"), crossed)
@@ -351,7 +351,7 @@
     inner = lax.ppermute(beside, "rows", evens)
     near = near_products(lefts, [payload, beside, above, below], 0)
     sources = [(index, 0) for index in range(2)]
-    return right_products(lefts, [inner, far], sources, order, 6 * LANES, near)
+    return right_products(lefts, [far, inner], sources, order, 6 * LANES, near)
 
 
 def general_plan(columns, counts, aggregate, matrix_blocks, payload, row_count, col_count):

time: 18.6 us -> 18.6 us (level)
  transfers between devices with their start and end apart: 5 -> 5, of which waited for: 1 -> 1; matrix products, arithmetic and copies ran while one was open for 0% -> 0% of each run, Pallas kernels for 41% -> 42%
where the time goes in v8:
time: 18.6 us; the launch traced here: 18.5 us
  Pallas kernels  10 us (54%)
  starting transfers between devices  7.33 us (39%)
  waiting for transfers between devices  1.07 us (6%)
    pallas_call x1, Pallas kernels, left_sums(): pl.pallas_call(functools.partial(left_kernel, order), out_shape=jax.Shape...  6.95 us
    ppermute x1, starting transfers between devices, paired_plan(): inner = lax.ppermute(beside, 'rows', evens)  2.69 us
    ppermute x1, starting transfers between devices, paired_plan(): beside = lax.ppermute(payload, 'cols', across)  2.13 us
    pallas_call x1, Pallas kernels, pack(): pl.pallas_call(pack_kernel, out_shape=jax.ShapeDtypeStruct((PAYLOAD, LANE...  1.17 us
    pallas_call x1, Pallas kernels, right_products(): pl.pallas_call(functools.partial(right_kernel, sources, order, first), ou...  1.16 us
    ppermute x1, starting transfers between devices, paired_plan(): below = lax.ppermute(payload, 'rows', ring)  1.1 us
    ppermute x1, waiting for transfers between devices, paired_plan(): far = lax.ppermute(payload, ('rows', 'cols'), crossed)  1.06 us
    ppermute x1, starting transfers between devices, paired_plan(): above = lax.ppermute(payload, 'rows', [(b, a) for a, b in ring])  0.96 us
  transfers between devices with their start and end apart: 5, of which 1 were waited for; matrix products, arithmetic and copies ran while one was open for 0% of the time, Pallas kernels for 42%

profile of v8, /device:TPU:1, one launch (start us, length us, event | category | flops | bytes accessed | tf_op | source)
XLA Modules:
  0.0 18.5 jit_solution(6540600344438608309)
XLA Ops:
  0.0 1.2 %pack_payload.1.payload_ref.refs_0_ = bf16[1040,128]{1,0:T(8,128)(2,1)S(1)} custom-call(s32[32]{0:T(128)} %aggregate_hbm.3, bf16[32,4096]{1,0:T(8,128)(2,1)} %restrict_hbm.1), custom_call_target="tpu_custom_call" | custom-call | tf_op jit(solution)/shard_map/pack_payload/pallas_call | solution.py:51
  1.2 2.1 %collective-permute-start = (bf16[1040,128]{1,0:T(8,128)(2,1)S(1)}, bf16[1040,128]{1,0:T(8,128)(2,1)S(1)}, u32[]{:S(2)}, u32[]{:S(2)}) collective-permute-start(bf16[1040,128]{1,0:T(8,128)(2,1)S(1)} %pack_payload.1.payload_ref.refs_0_), channel_id=1, source_target_pairs={{0,1},{1,0},{2,3},{3,2},{4,5},{5,4},{6,7},{7,6},{8,9},{9,8},{10,11... | collective-permute-start | bytes 798728 | tf_op jit(solution)/shard_map/ppermute | solution.py:346
  3.3 1.0 %collective-permute-start.3 = (bf16[1040,128]{1,0:T(8,128)(2,1)S(1)}, bf16[1040,128]{1,0:T(8,128)(2,1)S(1)}, u32[]{:S(2)}, u32[]{:S(2)}) collective-permute-start(bf16[1040,128]{1,0:T(8,128)(2,1)S(1)} %pack_payload.1.payload_ref.refs_0_), channel_id=1, source_target_pairs={{2,0},{4,2},{6,4},{8,6},{10,8},{12,10},{14,12},{16,14},{18,16},{20... | collective-permute-start | bytes 798728 | tf_op jit(solution)/shard_map/ppermute | solution.py:348
  4.3 1.1 %collective-permute-start.4 = (bf16[1040,128]{1,0:T(8,128)(2,1)S(1)}, bf16[1040,128]{1,0:T(8,128)(2,1)S(1)}, u32[]{:S(2)}, u32[]{:S(2)}) collective-permute-start(bf16[1040,128]{1,0:T(8,128)(2,1)S(1)} %pack_payload.1.payload_ref.refs_0_), channel_id=1, source_target_pairs={{0,2},{2,4},{4,6},{6,8},{8,10},{10,12},{12,14},{14,16},{16,18},{18... | collective-permute-start | bytes 798728 | tf_op jit(solution)/shard_map/ppermute | solution.py:347
  5.4 0.5 %collective-permute-start.1 = (bf16[1040,128]{1,0:T(8,128)(2,1)S(1)}, bf16[1040,128]{1,0:T(8,128)(2,1)S(1)}, u32[]{:S(2)}, u32[]{:S(2)}) collective-permute-start(bf16[1040,128]{1,0:T(8,128)(2,1)S(1)} %pack_payload.1.payload_ref.refs_0_), channel_id=1, source_target_pairs={{2,5},{3,4},{6,9},{7,8},{10,13},{11,12},{14,17},{15,16},{18,21},{1... | collective-permute-start | bytes 798728 | tf_op jit(solution)/shard_map/ppermute | solution.py:345
  5.8 6.9 %left_sums.1.lefts_ref = bf16[6,128,2048]{2,1,0:T(8,128)(2,1)S(1)} custom-call(s32[32,27]{1,0:T(8,128)} %columns_hbm.1, s32[32]{0:T(128)} %counts_hbm.1, s32[32]{0:T(128)} %aggregate_hbm.3, bf16[1040,128]{1,0:T(8,128)(2,1)S(1)} %pack_payload.1.payload_ref.refs_0_, bf16[2,16,64,1728]{3,2,1,0:T(8,128)(2,1)} %bitcast.1), custom_call_target="tpu_custom_call" | custom-call | flops 905969664 | bytes 2097152 | tf_op jit(solution)/shard_map/left_sums/pallas_call | solution.py:204
  12.8 0.0 collective-permute-done.refs_1_
  12.8 2.7 %collective-permute-start.2 = (bf16[1040,128]{1,0:T(8,128)(2,1)S(1)}, bf16[1040,128]{1,0:T(8,128)(2,1)S(1)}, u32[]{:S(2)}, u32[]{:S(2)}) collective-permute-start(bf16[1040,128]{1,0:T(8,128)(2,1)S(1)} %collective-permute-done.refs_1_), channel_id=1, source_target_pairs={{0,2},{2,0},{4,6},{6,4},{8,10},{10,8},{12,14},{14,12},{16,18},{18,... | collective-permute-start | bytes 798728 | tf_op jit(solution)/shard_map/ppermute | solution.py:351
  15.5 0.0 collective-permute-done.3.refs_2_
  15.5 0.0 collective-permute-done.4.refs_3_
  15.5 0.7 %near_products.1.refs_2_ = f32[4,2,64,128]{3,2,1,0:T(8,128)S(1)} custom-call(bf16[6,128,2048]{2,1,0:T(8,128)(2,1)S(1)} %left_sums.1.lefts_ref, bf16[1040,128]{1,0:T(8,128)(2,1)S(1)} %pack_payload.1.payload_ref.refs_0_, bf16[1040,128]{1,0:T(8,128)(2,1)S(1)} %collective-permute-done.refs_1_, bf16[1040,128]{1,0:T(8,128)(2,1)S(1)} %collective-permute-done.3.refs_2_, ...), custom_call_target="tpu_custom_call" | custom-call | flops 268435456 | bytes 262144 | tf_op jit(solution)/shard_map/near_products/pallas_call | solution.py:259
  16.2 1.1 %collective-permute-done.1.refs_0_ = bf16[1040,128]{1,0:T(8,128)(2,1)S(1)} collective-permute-done((bf16[1040,128]{1,0:T(8,128)(2,1)S(1)}, bf16[1040,128]{1,0:T(8,128)(2,1)S(1)}, u32[]{:S(2)}, u32[]{:S(2)}) %collective-permute-start.1) | collective-permute-done | bytes 266272 | tf_op jit(solution)/shard_map/ppermute | solution.py:345
  17.3 0.0 collective-permute-done.2.refs_1_
  17.3 1.2 %right_products.1 = f32[2,64,768]{2,1,0:T(8,128)} custom-call(bf16[6,128,2048]{2,1,0:T(8,128)(2,1)S(1)} %left_sums.1.lefts_ref, bf16[1040,128]{1,0:T(8,128)(2,1)S(1)} %collective-permute-done.1.refs_0_, bf16[1040,128]{1,0:T(8,128)(2,1)S(1)} %collective-permute-done.2.refs_1_, f32[4,2,64,128]{3,2,1,0:T(8,128)S(1)} %near_products.1.refs_2_), custom_call_target="tpu_custom_call" | custom-call | flops 134217728 | bytes 131072 | tf_op jit(solution)/shard_map/right_products/pallas_call | solution.py:308
Async XLA Ops:
  1.2 11.6 %collective-permute-start = (bf16[1040,128]{1,0:T(8,128)(2,1)S(1)}, bf16[1040,128]{1,0:T(8,128)(2,1)S(1)}, u32[]{:S(2)}, u32[]{:S(2)}) collective-permute-start(bf16[1040,128]{1,0:T(8,128)(2,1)S(1)} %pack_payload.1.payload_ref.refs_0_), channel_id=1, source_target_pairs={{0,1},{1,0},{2,3},{3,2},{4,5},{5,4},{6,7},{7,6},{8,9},{9,8},{10,11... | collective-permute-start | bytes 798728 | tf_op jit(solution)/shard_map/ppermute | solution.py:346
  3.3 12.2 %collective-permute-start.3 = (bf16[1040,128]{1,0:T(8,128)(2,1)S(1)}, bf16[1040,128]{1,0:T(8,128)(2,1)S(1)}, u32[]{:S(2)}, u32[]{:S(2)}) collective-permute-start(bf16[1040,128]{1,0:T(8,128)(2,1)S(1)} %pack_payload.1.payload_ref.refs_0_), channel_id=1, source_target_pairs={{2,0},{4,2},{6,4},{8,6},{10,8},{12,10},{14,12},{16,14},{18,16},{20... | collective-permute-start | bytes 798728 | tf_op jit(solution)/shard_map/ppermute | solution.py:348
  4.3 11.2 %collective-permute-start.4 = (bf16[1040,128]{1,0:T(8,128)(2,1)S(1)}, bf16[1040,128]{1,0:T(8,128)(2,1)S(1)}, u32[]{:S(2)}, u32[]{:S(2)}) collective-permute-start(bf16[1040,128]{1,0:T(8,128)(2,1)S(1)} %pack_payload.1.payload_ref.refs_0_), channel_id=1, source_target_pairs={{0,2},{2,4},{4,6},{6,8},{8,10},{10,12},{12,14},{14,16},{16,18},{18... | collective-permute-start | bytes 798728 | tf_op jit(solution)/shard_map/ppermute | solution.py:347
  5.4 11.9 %collective-permute-start.1 = (bf16[1040,128]{1,0:T(8,128)(2,1)S(1)}, bf16[1040,128]{1,0:T(8,128)(2,1)S(1)}, u32[]{:S(2)}, u32[]{:S(2)}) collective-permute-start(bf16[1040,128]{1,0:T(8,128)(2,1)S(1)} %pack_payload.1.payload_ref.refs_0_), channel_id=1, source_target_pairs={{2,5},{3,4},{6,9},{7,8},{10,13},{11,12},{14,17},{15,16},{18,21},{1... | collective-permute-start | bytes 798728 | tf_op jit(solution)/shard_map/ppermute | solution.py:345
  12.8 4.5 %collective-permute-start.2 = (bf16[1040,128]{1,0:T(8,128)(2,1)S(1)}, bf16[1040,128]{1,0:T(8,128)(2,1)S(1)}, u32[]{:S(2)}, u32[]{:S(2)}) collective-permute-start(bf16[1040,128]{1,0:T(8,128)(2,1)S(1)} %collective-permute-done.refs_1_), channel_id=1, source_target_pairs={{0,2},{2,0},{4,6},{6,4},{8,10},{10,8},{12,14},{14,12},{16,18},{18,... | collective-permute-start | bytes 798728 | tf_op jit(solution)/shard_map/ppermute | solution.py:351
